TPU v7x, 32 devices: a whole 2x2x4 slice. The times are simulated.
32 devices in a mesh: row: 8 (over y, x, core), col: 4 (over z).
Axes of the slice: x: 2, y: 2, z: 4, core: 2. Of those that a mesh axis runs over, the one named last changes fastest.
Arguments:
- features: bfloat16 [32, 1024, 1024], P(None, 'row', 'col'), may hold values from -45 to 45
- first_kernel: bfloat16 [3, 3, 32, 32], replicated, may hold values from -0.375 to 0.375
- second_kernel: bfloat16 [3, 3, 32, 32], replicated, may hold values from -0.375 to 0.375
- first_gain: float32 [32], replicated, may hold values from 0.5 to 1.5
- first_shift: float32 [32], replicated, may hold values from -3 to 3
- second_gain: float32 [32], replicated, may hold values from 0.5 to 1.5
- second_shift: float32 [32], replicated, may hold values from -3 to 3
Outputs:
- symmetric_map: bfloat16 [32, 1024, 1024], P(None, 'row', 'col')
All inputs are finite; a program needn't handle non-finite values.
Results may differ from a plain program's by a relative error of at most 0.0053.
Values may be sent and summed in bfloat16 or wider, within the bound.
A program may use at most 192 MiB of HBM per device.

v0:
```python
import functools

import jax
import jax.numpy as jnp
from jax import lax
from jax.experimental import pallas as pl
from jax.experimental.pallas import tpu as pltpu
from jax.sharding import PartitionSpec as P

STEP = 8
GROUP = 4
EPSILON = 1e-05
LANES = 128
MESH = pl.DeviceIdType.MESH


def iota(dim):
    return lax.broadcasted_iota(jnp.int32, (LANES, LANES), dim)


def one_hot(mask):
    return jnp.where(mask, 1.0, 0.0).astype(jnp.bfloat16)


def dot(a, b):
    return jnp.dot(a, b, preferred_element_type=jnp.float32)


def block_kernel(
    rows,
    cols,
    x_ref,
    first_ref,
    second_ref,
    scales_ref,
    out_ref,
    pad_one,
    pad_two,
    hidden,
    packed,
    strips,
    col_stats,
    row_stats,
    row_send,
    row_recv,
    col_send,
    col_recv,
    cs_send,
    cs_recv,
    rs_send,
    rs_recv,
):
    row = lax.axis_index("row")
    col = lax.axis_index("col")
    phases, depth, width = x_ref.shape
    chans = scales_ref.shape[1]
    count = depth // chans
    full = depth + 2 * chans
    cells = float(phases * count * width)
    centre = pl.ds(LANES, width)

    barrier = pltpu.get_barrier_semaphore()
    for d in range(1, cols):
        pl.semaphore_signal(
            barrier, inc=1, device_id=(row, lax.rem(col + d, cols)), device_id_type=MESH
        )
    for d in range(1, rows):
        pl.semaphore_signal(
            barrier, inc=1, device_id=(lax.rem(row + d, rows), col), device_id_type=MESH
        )
    pl.semaphore_wait(barrier, rows + cols - 2)

    def row_copy(pad, n, down):
        source = depth if down else chans
        target = 0 if down else depth + chans
        device = jnp.minimum(row + 1, rows - 1) if down else jnp.maximum(row - 1, 0)
        slot = 2 * n + int(down)
        return pltpu.make_async_remote_copy(
            src_ref=pad.at[:, pl.ds(source, chans), centre],
            dst_ref=pad.at[:, pl.ds(target, chans), centre],
            send_sem=row_send.at[slot],
            recv_sem=row_recv.at[slot],
            device_id=(device, col),
            device_id_type=MESH,
        )

    def col_copy(n, right):
        device = jnp.minimum(col + 1, cols - 1) if right else jnp.maximum(col - 1, 0)
        slot = 2 * n + int(right)
        return pltpu.make_async_remote_copy(
            src_ref=packed.at[n],
            dst_ref=strips.at[slot],
            send_sem=col_send.at[slot],
            recv_sem=col_recv.at[slot],
            device_id=(row, device),
            device_id_type=MESH,
        )

    def halo(pad, n):
        up, down = row_copy(pad, n, False), row_copy(pad, n, True)
        left, right = col_copy(n, False), col_copy(n, True)
        has_up, has_down = row > 0, row < rows - 1
        has_left, has_right = col > 0, col < cols - 1

        @pl.when(has_up)
        def _():
            up.start()

        @pl.when(has_down)
        def _():
            down.start()

        blank = jnp.zeros((phases, chans, width), jnp.bfloat16)

        @pl.when(jnp.logical_not(has_up))
        def _():
            pad[:, pl.ds(0, chans), centre] = blank

        @pl.when(jnp.logical_not(has_down))
        def _():
            pad[:, pl.ds(depth + chans, chans), centre] = blank

        @pl.when(jnp.logical_not(has_left))
        def _():
            strips[2 * n + 1] = jnp.zeros((full, LANES), jnp.bfloat16)

        @pl.when(jnp.logical_not(has_right))
        def _():
            strips[2 * n] = jnp.zeros((full, LANES), jnp.bfloat16)

        @pl.when(has_up)
        def _():
            down.wait_recv()
            up.wait_send()

        @pl.when(has_down)
        def _():
            up.wait_recv()
            down.wait_send()

        total = jnp.zeros((full, LANES), jnp.float32)
        i, j = iota(0), iota(1)
        edge = LANES - STEP
        for phase in range(phases):
            at = phase * STEP
            tail = one_hot((i >= edge) & (j == i - edge + at))
            head = one_hot((i < STEP) & (j == i + LANES // 2 + at))
            total += dot(pad[phase, :, pl.ds(width, LANES)], tail)
            total += dot(pad[phase, :, pl.ds(LANES, LANES)], head)
        packed[n] = total.astype(jnp.bfloat16)

        @pl.when(has_left)
        def _():
            left.start()

        @pl.when(has_right)
        def _():
            right.start()

        @pl.when(has_left)
        def _():
            right.wait_recv()
            left.wait_send()

        @pl.when(has_right)
        def _():
            left.wait_recv()
            right.wait_send()

        for phase in range(phases):
            at = phase * STEP
            tail = one_hot((j >= edge) & (i == j - edge + at))
            head = one_hot((j < STEP) & (i == j + LANES // 2 + at))
            pad[phase, :, pl.ds(0, LANES)] = dot(strips[2 * n + 1], tail).astype(jnp.bfloat16)
            pad[phase, :, pl.ds(width + LANES, LANES)] = dot(strips[2 * n], head).astype(
                jnp.bfloat16
            )

    def fold(values):
        total = jnp.sum(values.reshape(-1, chans, width), axis=0)
        return sum(total[:, k : k + LANES] for k in range(0, width, LANES))

    def conv(pad, weights):
        def body(phase, acc):
            shifted = [
                pad[phase, :, pl.ds(LANES + (b - 1) * STEP, width)] for b in range(3)
            ]
            for g in range(count // GROUP):
                low = g * GROUP * chans
                high = low + (GROUP + 2) * chans
                stacked = jnp.concatenate([s[low:high] for s in shifted], axis=0)
                part = dot(weights[...], stacked)
                hidden[phase, pl.ds(low, GROUP * chans), :] = part
                acc = acc + fold(part)
            return acc

        return lax.fori_loop(0, phases, body, jnp.zeros((chans, LANES), jnp.float32))

    def merge(own, other, size, stats, send, recv, n, axis_size, along_row):
        base = n * axis_size
        stats[base, pl.ds(0, chans), :] = own
        stats[base, pl.ds(chans, chans), :] = other
        copies = []
        for d in range(1, axis_size):
            device = (
                (lax.rem(row + d, axis_size), col)
                if along_row
                else (row, lax.rem(col + d, axis_size))
            )
            copy = pltpu.make_async_remote_copy(
                src_ref=stats.at[base],
                dst_ref=stats.at[base + d],
                send_sem=send.at[base + d],
                recv_sem=recv.at[base + d],
                device_id=device,
                device_id_type=MESH,
            )
            copy.start()
            copies.append(copy)
        for copy in copies:
            copy.wait()
        means = [stats[base + d, pl.ds(0, chans), :] for d in range(axis_size)]
        mean = sum(means) / axis_size
        squares = sum(stats[base + d, pl.ds(chans, chans), :] for d in range(axis_size))
        spread = sum((m - mean) * (m - mean) for m in means)
        return mean, squares + size * spread

    def norm(acc, n):
        own = jnp.broadcast_to(jnp.sum(acc, axis=1, keepdims=True) / cells, (chans, LANES))
        wide = jnp.concatenate([own] * (width // LANES), axis=1)

        def body(phase, squares):
            for q in range(count):
                diff = hidden[phase, pl.ds(q * chans, chans), :] - wide
                squares = squares + fold(diff * diff)
            return squares

        squares = lax.fori_loop(0, phases, body, jnp.zeros((chans, LANES), jnp.float32))
        squares = jnp.broadcast_to(jnp.sum(squares, axis=1, keepdims=True), (chans, LANES))
        mean, squares = merge(
            own, squares, cells, col_stats, cs_send, cs_recv, n, cols, False
        )
        mean, squares = merge(
            mean, squares, cells * cols, row_stats, rs_send, rs_recv, n, rows, True
        )
        factor = scales_ref[2 * n] * lax.rsqrt(squares / (cells * (rows * cols)) + EPSILON)
        shift = scales_ref[2 * n + 1]
        repeat = lambda v: jnp.concatenate([v] * (width // LANES), axis=1)
        return repeat(mean), repeat(factor), repeat(shift)

    pad_one[:, pl.ds(chans, depth), centre] = x_ref[...]
    halo(pad_one, 0)
    mean, factor, shift = norm(conv(pad_one, first_ref), 0)

    def activate(phase, carry):
        for q in range(count):
            cell = hidden[phase, pl.ds(q * chans, chans), :]
            cell = jnp.maximum((cell - mean) * factor + shift, 0.0)
            pad_two[phase, pl.ds((q + 1) * chans, chans), centre] = cell.astype(jnp.bfloat16)
        return carry

    lax.fori_loop(0, phases, activate, 0)
    halo(pad_two, 1)
    mean, factor, shift = norm(conv(pad_two, second_ref), 1)

    def finish(phase, carry):
        for q in range(count):
            at = pl.ds(q * chans, chans)
            cell = (hidden[phase, at, :] - mean) * factor + shift
            out_ref[phase, at, :] = (x_ref[phase, at, :].astype(jnp.float32) + cell).astype(
                jnp.bfloat16
            )
        return carry

    lax.fori_loop(0, phases, finish, 0)


def banded(kernel):
    taps = jnp.transpose(kernel, (2, 1, 0, 3))
    rows = [
        jnp.pad(taps, ((0, 0), (0, 0), (q, GROUP - 1 - q), (0, 0))) for q in range(GROUP)
    ]
    return jnp.stack(rows).reshape(GROUP * kernel.shape[2], -1)


def residual_block(rows, cols, features, first, second, scales):
    chans, height, width = features.shape
    count = height // STEP
    depth = count * chans
    x = jnp.transpose(features.reshape(chans, count, STEP, width), (2, 1, 0, 3))
    x = x.reshape(STEP, depth, width)
    full = depth + 2 * chans
    scales = jnp.broadcast_to(jnp.stack(scales)[:, :, None], (4, chans, LANES))
    vmem = pl.BlockSpec(memory_space=pltpu.VMEM)
    dma = pltpu.SemaphoreType.DMA
    summed = pl.pallas_call(
        functools.partial(block_kernel, rows, cols),
        out_shape=jax.ShapeDtypeStruct(x.shape, jnp.bfloat16),
        in_specs=[vmem] * 4,
        out_specs=vmem,
        scratch_shapes=[
            pltpu.VMEM((STEP, full, width + 2 * LANES), jnp.bfloat16),
            pltpu.VMEM((STEP, full, width + 2 * LANES), jnp.bfloat16),
            pltpu.VMEM((STEP, depth, width), jnp.float32),
            pltpu.VMEM((2, full, LANES), jnp.bfloat16),
            pltpu.VMEM((4, full, LANES), jnp.bfloat16),
            pltpu.VMEM((2 * cols, 2 * chans, LANES), jnp.float32),
            pltpu.VMEM((2 * rows, 2 * chans, LANES), jnp.float32),
            dma((4,)),
            dma((4,)),
            dma((4,)),
            dma((4,)),
            dma((2 * cols,)),
            dma((2 * cols,)),
            dma((2 * rows,)),
            dma((2 * rows,)),
        ],
        compiler_params=pltpu.CompilerParams(
            collective_id=0, has_side_effects=True, vmem_limit_bytes=48 * 1024 * 1024
        ),
    )(x, banded(first), banded(second), scales)
    summed = summed.reshape(STEP, count, chans, width)
    return jnp.transpose(summed, (2, 1, 0, 3)).reshape(features.shape)


def mirror_kernel(
    rows, cols, chunks, s_ref, out_ref, got, relay, send, recv, relay_send, relay_recv
):
    row = lax.axis_index("row")
    col = lax.axis_index("col")
    ratio = rows // cols
    chans, height, _ = s_ref.shape
    pieces = len(chunks)
    block = lax.div(row, ratio)
    part = lax.rem(row, ratio)
    relays = block == col

    barrier = pltpu.get_barrier_semaphore()
    for d in range(1, cols):
        pl.semaphore_signal(
            barrier, inc=1, device_id=(row, lax.rem(col + d, cols)), device_id_type=MESH
        )
    for d in range(1, rows):
        pl.semaphore_signal(
            barrier, inc=1, device_id=(lax.rem(row + d, rows), col), device_id_type=MESH
        )
    for h in range(ratio):

        @pl.when(jnp.logical_not(relays))
        def _(h=h):
            pl.semaphore_signal(
                barrier, inc=1, device_id=(ratio * col + h, block), device_id_type=MESH
            )

    pl.semaphore_wait(barrier, rows + cols - 2 + jnp.where(relays, 0, ratio))

    def direct(source_col, source_block):
        z, p = lax.rem(source_col, 4), lax.rem(source_block, 4)
        chosen = (z == p) & (lax.rem(source_col + source_block, 8) < 4)
        for a, b in DIRECT:
            chosen = chosen | ((z == a) & (p == b))
        return chosen

    mine = direct(col, block)

    def span(k):
        low, size = chunks[k]
        return pl.ds(low, size)

    def source(h, k):
        return s_ref.at[span(k), :, pl.ds(h * height, height)]

    def straight(h, k):
        return pltpu.make_async_remote_copy(
            src_ref=source(h, k),
            dst_ref=got.at[part, span(k)],
            send_sem=send.at[h * pieces + k],
            recv_sem=recv.at[part * pieces + k],
            device_id=(ratio * col + h, block),
            device_id_type=MESH,
        )

    def arrive(j, k):
        return pltpu.make_async_remote_copy(
            src_ref=got.at[j, span(k)],
            dst_ref=got.at[j, span(k)],
            send_sem=send.at[j * pieces + k],
            recv_sem=recv.at[j * pieces + k],
            device_id=(row, col),
            device_id_type=MESH,
        )

    def first_leg(h, k):
        slot = (lax.rem(block - col + cols, cols) - 1) * ratio + part
        return pltpu.make_async_remote_copy(
            src_ref=source(h, k),
            dst_ref=relay.at[slot, span(k)],
            send_sem=send.at[h * pieces + k],
            recv_sem=relay_recv.at[slot * pieces + k],
            device_id=(ratio * col + h, col),
            device_id_type=MESH,
        )

    def second_leg(d, e, k):
        slot = (d - 1) * ratio + e
        return pltpu.make_async_remote_copy(
            src_ref=relay.at[slot, span(k)],
            dst_ref=got.at[e, span(k)],
            send_sem=relay_send.at[slot * pieces + k],
            recv_sem=recv.at[e * pieces + k],
            device_id=(row, lax.rem(col + d, cols)),
            device_id_type=MESH,
        )

    @pl.when(jnp.logical_not(relays) & mine)
    def _():
        for k in range(pieces):
            for h in range(ratio):
                straight(h, k).start()

    @pl.when(jnp.logical_not(relays | mine))
    def _():
        for k in range(pieces):
            for h in range(ratio):
                first_leg(h, k).start()

    @pl.when(relays)
    def _():
        for h in range(ratio):

            @pl.when(part != h)
            def _(h=h):
                for k in range(pieces):
                    straight(h, k).start()

            @pl.when(part == h)
            def _(h=h):
                got[h] = s_ref[:, :, h * height : (h + 1) * height]

        for k in range(pieces):
            for d in range(1, cols):

                @pl.when(jnp.logical_not(direct(col, lax.rem(col + d, cols))))
                def _(d=d, k=k):
                    for e in range(ratio):
                        slot = (d - 1) * ratio + e
                        pltpu.make_async_remote_copy(
                            src_ref=relay.at[slot, span(k)],
                            dst_ref=relay.at[slot, span(k)],
                            send_sem=relay_send.at[slot * pieces + k],
                            recv_sem=relay_recv.at[slot * pieces + k],
                            device_id=(row, col),
                            device_id_type=MESH,
                        ).wait_recv()
                        second_leg(d, e, k).start()

    for k in range(pieces):
        for j in range(ratio):

            @pl.when(jnp.logical_not(relays & (part == j)))
            def _(j=j, k=k):
                arrive(j, k).wait_recv()

            low, size = chunks[k]
            at = pl.ds(j * height, height)

            def body(c, carry, j=j, at=at):
                turned = jnp.swapaxes(got[j, c].astype(jnp.float32), 0, 1)
                total = s_ref[c, :, at].astype(jnp.float32) + turned
                out_ref[c, :, at] = (total * 0.5).astype(jnp.bfloat16)
                return carry

            lax.fori_loop(low, low + size, body, 0)

    for k in range(pieces):
        for h in range(ratio):

            @pl.when(jnp.logical_not(relays & (part == h)))
            def _(h=h, k=k):
                straight(h, k).wait_send()

    @pl.when(relays)
    def _():
        for k in range(pieces):
            for d in range(1, cols):

                @pl.when(jnp.logical_not(direct(col, lax.rem(col + d, cols))))
                def _(d=d, k=k):
                    for e in range(ratio):
                        second_leg(d, e, k).wait_send()


DIRECT = ((0, 1), (0, 2), (1, 3), (2, 0), (3, 1), (3, 2))


def symmetrize(rows, cols, summed):
    chans, height, width = summed.shape
    ratio = rows // cols
    size = 4 if chans % 4 == 0 else chans
    chunks = tuple((low, size) for low in range(0, chans, size))
    pieces = len(chunks)
    slots = (cols - 1) * ratio
    vmem = pl.BlockSpec(memory_space=pltpu.VMEM)
    dma = pltpu.SemaphoreType.DMA
    return pl.pallas_call(
        functools.partial(mirror_kernel, rows, cols, chunks),
        out_shape=jax.ShapeDtypeStruct(summed.shape, jnp.bfloat16),
        in_specs=[vmem],
        out_specs=vmem,
        scratch_shapes=[
            pltpu.VMEM((ratio, chans, height, height), jnp.bfloat16),
            pltpu.VMEM((slots, chans, height, height), jnp.bfloat16),
            dma((ratio * pieces,)),
            dma((ratio * pieces,)),
            dma((slots * pieces,)),
            dma((slots * pieces,)),
        ],
        compiler_params=pltpu.CompilerParams(
            collective_id=1, has_side_effects=True, vmem_limit_bytes=48 * 1024 * 1024
        ),
    )(summed)


def solution(mesh):
    rows, cols = mesh.shape["row"], mesh.shape["col"]

    def per_device(features, first, second, gain_one, shift_one, gain_two, shift_two):
        scales = (gain_one, shift_one, gain_two, shift_two)
        summed = residual_block(rows, cols, features, first, second, scales)
        return symmetrize(rows, cols, summed)

    placed = (P(None, "row", "col"), P(), P(), P(), P(), P(), P())
    return jax.shard_map(
        per_device, mesh=mesh, in_specs=placed, out_specs=P(None, "row", "col"), check_vma=False
    )
```

profile of v0, /device:TPU:1, one launch (start us, length us, event | category | flops | bytes accessed | tf_op | source)
XLA Modules:
  0.0 130.9 jit_solution(7322063152138313404)
XLA Ops:
  0.0 0.7 pad_maximum_fusion.2
  0.7 0.1 broadcast_in_dim.2.scales_ref
  0.8 0.0 copy-start.1
  0.8 1.1 pad_bitcast_fusion.7
  1.9 0.2 pad_maximum_fusion
  2.1 0.3 copy.18
  2.4 0.4 reshape.25.first_ref
  2.8 0.0 copy-done.1
  2.8 0.0 copy-start
  2.8 0.1 pad_bitcast_fusion.3
  2.9 0.2 pad_maximum_fusion.1
  3.1 0.3 copy.19
  3.3 0.4 reshape.26.second_ref
  3.8 0.6 copy-done
  4.4 1.2 copy.12
  5.6 64.4 %shard_map.73 = bf16[8,512,256]{2,1,0:T(8,128)(2,1)S(1)} custom-call(bf16[8,512,256]{2,1,0:T(8,128)(2,1)S(1)} %bitcast.33, bf16[128,576]{1,0:T(8,128)(2,1)S(1)} %reshape.25.first_ref, bf16[128,576]{1,0:T(8,128)(2,1)S(1)} %reshape.26.second_ref, f32[4,32,128]{2,1,0:T(8,128)S(1)} %broadcast_in_dim.2.scales_ref), custom_call_target="tpu_custom_call" | custom-call | tf_op jit(solution)/shard_map/pallas_call | solution.py:296
  70.0 1.2 copy.23
  71.2 58.4 %shard_map.74 = bf16[32,128,256]{2,1,0:T(8,128)(2,1)S(1)} custom-call(bf16[32,128,256]{2,1,0:T(8,128)(2,1)S(1)} %bitcast.34), custom_call_target="tpu_custom_call" | custom-call | tf_op jit(solution)/shard_map/pallas_call | solution.py:505
  129.6 1.3 %copy.25 = bf16[32,128,256]{2,1,0:T(8,128)(2,1)} copy(bf16[32,128,256]{2,1,0:T(8,128)(2,1)S(1)} %shard_map.74) | data formatting | bytes 4194304
Async XLA Ops:
  0.8 2.0 %copy-start.1 = (bf16[3,3,32,32]{3,2,1,0:T(8,128)(2,1)S(1)}, bf16[3,3,32,32]{3,2,1,0:T(8,128)(2,1)}, u32[]{:S(2)}) copy-start(bf16[3,3,32,32]{3,2,1,0:T(8,128)(2,1)} %param.9) | copy-start | bytes 55300
  2.8 1.6 %copy-start = (bf16[32,128,256]{2,1,0:T(8,128)(2,1)S(1)}, bf16[32,128,256]{2,1,0:T(8,128)(2,1)}, u32[]{:S(2)}) copy-start(bf16[32,128,256]{2,1,0:T(8,128)(2,1)} %param.7) | copy-start | bytes 6291460
where the time goes:
time: 131 us
  Pallas kernels  123 us (94%)
  local copies, waits for them, and re-layouts  6.95 us (5%)
    pallas_call x1, Pallas kernels, residual_block(): pl.pallas_call(functools.partial(block_kernel, rows, cols), out_shape=jax...  64.4 us
    pallas_call x1, Pallas kernels, symmetrize(): pl.pallas_call(functools.partial(mirror_kernel, rows, cols, chunks), out_...  58.4 us

commit v1 on v0

v1 whole, which is shorter than its diff:
```python
import functools

import jax
import jax.numpy as jnp
from jax import lax
from jax.experimental import pallas as pl
from jax.experimental.pallas import tpu as pltpu
from jax.sharding import PartitionSpec as P

STEP = 8
GROUP = 4
EPSILON = 1e-05
LANES = 128
PART = 16
MESH = pl.DeviceIdType.MESH
BF16 = jnp.bfloat16
F32 = jnp.float32

DIRECT = ((0, 1), (0, 2), (1, 3), (2, 0), (3, 1), (3, 2))

WAYS = ((-1, -1), (-1, 0), (-1, 1), (0, -1), (0, 1), (1, -1), (1, 0), (1, 1))


def iota(shape, dim):
    return lax.broadcasted_iota(jnp.int32, shape, dim)


def one_hot(mask):
    return jnp.where(mask, 1.0, 0.0).astype(BF16)


def dot(a, b):
    return jnp.dot(a, b, preferred_element_type=F32)


def remote(src, dst, send, recv, device):
    return pltpu.make_async_remote_copy(
        src_ref=src,
        dst_ref=dst,
        send_sem=send,
        recv_sem=recv,
        device_id=device,
        device_id_type=MESH,
    )


def kernel(
    rows,
    cols,
    x_ref,
    first_ref,
    second_ref,
    gain_one,
    shift_one,
    gain_two,
    shift_two,
    out_ref,
    pad_one,
    pad_two,
    hidden,
    pack_sel,
    unpack_sel,
    weights,
    packed,
    strips,
    col_stats,
    row_stats,
    summed,
    got,
    wide,
    relay,
    halo_send,
    halo_recv,
    cs_send,
    cs_recv,
    rs_send,
    rs_recv,
    send,
    recv,
    relay_send,
    relay_recv,
):
    row = lax.axis_index("row")
    col = lax.axis_index("col")
    phases, depth, width = x_ref.shape
    chans, height, _ = out_ref.shape
    count = depth // chans
    full = depth + 2 * chans
    fold_rows = depth // 2
    half_lanes = LANES // 2
    cells = float(phases * count * width)
    centre = pl.ds(LANES, width)
    ratio = rows // cols
    block = lax.div(row, ratio)
    part = lax.rem(row, ratio)
    relays = block == col
    parts = chans // PART
    pieces = parts * phases

    for pad in (pad_one, pad_two):
        pad[:, pl.ds(0, chans), :] = jnp.zeros((phases, chans, width + 2 * LANES), BF16)
        pad[:, pl.ds(depth + chans, chans), :] = jnp.zeros(
            (phases, chans, width + 2 * LANES), BF16
        )
    strips[...] = jnp.zeros_like(strips)

    barrier = pltpu.get_barrier_semaphore()

    def greet(device):
        pl.semaphore_signal(barrier, inc=1, device_id=device, device_id_type=MESH)

    def neighbour(k):
        dr, dc = WAYS[k]
        there = jnp.bool_(True)
        if dr:
            there = there & ((row > 0) if dr < 0 else (row < rows - 1))
        if dc:
            there = there & ((col > 0) if dc < 0 else (col < cols - 1))
        device = (jnp.clip(row + dr, 0, rows - 1), jnp.clip(col + dc, 0, cols - 1))
        return there, device

    expected = jnp.int32(rows + cols - 2)
    for d in range(1, cols):
        greet((row, lax.rem(col + d, cols)))
    for d in range(1, rows):
        greet((lax.rem(row + d, rows), col))
    for k in (0, 2, 5, 7):
        there, device = neighbour(k)
        pl.when(there)(functools.partial(greet, device))
        expected = expected + jnp.where(there, 1, 0)
    for h in range(ratio):
        pl.when(jnp.logical_not(relays))(functools.partial(greet, (ratio * col + h, block)))
    expected = expected + jnp.where(relays, 0, ratio)

    pad_one[:, pl.ds(chans, depth), centre] = x_ref[...]

    i, j = iota((2 * LANES, LANES), 0), iota((2 * LANES, LANES), 1)
    in_half, source_lane = i // LANES, i % LANES
    edge = LANES - STEP
    for phase in range(phases):
        at = in_half * half_lanes + phase * STEP
        pack_sel[phase] = one_hot((source_lane < STEP) & (j == source_lane + at))
        pack_sel[phases + phase] = one_hot((source_lane >= edge) & (j == source_lane - edge + at))
    i, j = iota((LANES, 2 * LANES), 0), iota((LANES, 2 * LANES), 1)
    in_half, target_lane = j // LANES, j % LANES
    for phase in range(phases):
        at = in_half * half_lanes + phase * STEP
        unpack_sel[phase] = one_hot((target_lane >= edge) & (i == target_lane - edge + at))
        unpack_sel[phases + phase] = one_hot((target_lane < STEP) & (i == target_lane + at))

    def band(n, kernel_ref):
        span = (GROUP + 2) * chans
        c, k = iota((chans, span), 0), iota((chans, span), 1)
        for q in range(GROUP):
            for b in range(3):
                total = jnp.zeros((chans, span), F32)
                for a in range(3):
                    total += dot(kernel_ref[a, b], one_hot(k == c + (q + a) * chans))
                weights[n, b, pl.ds(q * chans, chans), :] = total.astype(BF16)

    pl.semaphore_wait(barrier, expected)

    def halo_copy(pad, n, k):
        dr, dc = WAYS[k]
        there, device = neighbour(k)
        if dc == 0:
            source = chans if dr < 0 else depth
            target = depth + chans if dr < 0 else 0
            src = pad.at[:, pl.ds(source, chans), centre]
            dst = pad.at[:, pl.ds(target, chans), centre]
        else:
            mine, theirs = (0, 1) if dc < 0 else (1, 0)
            if dr == 0:
                src = packed.at[n, mine]
                dst = strips.at[n, theirs, pl.ds(0, fold_rows)]
            elif dr < 0:
                src = packed.at[n, mine, pl.ds(0, chans)]
                dst = strips.at[n, theirs, pl.ds(fold_rows + chans, chans)]
            else:
                src = packed.at[n, mine, pl.ds(fold_rows - chans, chans)]
                dst = strips.at[n, theirs, pl.ds(fold_rows, chans)]
        slot = n * 8 + k
        return there, remote(src, dst, halo_send.at[slot], halo_recv.at[slot], device)

    def halo_start(pad, n):
        for k in (1, 6):
            there, copy = halo_copy(pad, n, k)
            pl.when(there)(copy.start)
        for side, lane in ((0, LANES), (1, width)):
            total = jnp.zeros((fold_rows, LANES), F32)
            for phase in range(phases):
                low = pad[phase, pl.ds(chans, fold_rows), pl.ds(lane, LANES)]
                high = pad[phase, pl.ds(chans + fold_rows, fold_rows), pl.ds(lane, LANES)]
                total += dot(
                    jnp.concatenate([low, high], axis=1), pack_sel[side * phases + phase]
                )
            packed[n, side] = total.astype(BF16)
            for k in (3, 0, 5) if side == 0 else (4, 2, 7):
                there, copy = halo_copy(pad, n, k)
                pl.when(there)(copy.start)

    def halo_finish(pad, n):
        for k in range(8):
            there, copy = halo_copy(pad, n, k)
            _, back = halo_copy(pad, n, 7 - k)

            @pl.when(there)
            def _(copy=copy, back=back):
                back.wait_recv()
                copy.wait_send()

        for side, lane in ((0, 0), (1, width + LANES)):
            at = pl.ds(lane, LANES)

            def body(phase, carry, side=side, at=at):
                placed = dot(strips[n, side], unpack_sel[side * phases + phase]).astype(BF16)
                pad[phase, pl.ds(chans, fold_rows), at] = placed[:fold_rows, :LANES]
                pad[phase, pl.ds(chans + fold_rows, fold_rows), at] = placed[:fold_rows, LANES:]
                pad[phase, pl.ds(0, chans), at] = placed[fold_rows : fold_rows + chans, LANES:]
                pad[phase, pl.ds(full - chans, chans), at] = placed[fold_rows + chans :, :LANES]
                return carry

            lax.fori_loop(0, phases, body, 0, unroll=4)

    tiles = width // LANES

    def held(at):
        return jnp.concatenate([hidden[k, at, :] for k in range(tiles)], axis=1)

    def keep(at, values):
        for k in range(tiles):
            hidden[k, at, :] = values[:, k * LANES : (k + 1) * LANES]

    def fold(values):
        total = jnp.sum(values.reshape(-1, chans, width), axis=0)
        return sum(total[:, k : k + LANES] for k in range(0, width, LANES))

    def conv(pad, n):
        def body(phase, acc):
            shifted = [
                pad[phase, :, pl.ds(LANES + (b - 1) * STEP, width)] for b in range(3)
            ]
            for g in range(count // GROUP):
                low = g * GROUP * chans
                high = low + (GROUP + 2) * chans
                result = sum(dot(weights[n, b], shifted[b][low:high]) for b in range(3))
                keep(pl.ds(phase * depth + low, GROUP * chans), result)
                acc = acc + fold(result)
            return acc

        return lax.fori_loop(0, phases, body, jnp.zeros((chans, LANES), F32), unroll=2)

    square = (chans, LANES)
    diagonal = iota(square, 0) == iota(square, 1)

    def to_lanes(values):
        return jnp.sum(jnp.where(diagonal, values, 0.0), axis=0, keepdims=True)

    def to_rows(values):
        spread = jnp.where(diagonal, jnp.broadcast_to(values, square), 0.0)
        return jnp.broadcast_to(jnp.sum(spread, axis=1, keepdims=True), square)

    def merge(own, other, size, stats, sends, recvs, n, axis_size, along_row):
        base = n * axis_size
        stats[base, pl.ds(0, 1), :] = own
        stats[base, pl.ds(1, 1), :] = other
        copies = []
        for d in range(1, axis_size):
            device = (
                (lax.rem(row + d, axis_size), col)
                if along_row
                else (row, lax.rem(col + d, axis_size))
            )
            copy = remote(
                stats.at[base],
                stats.at[base + d],
                sends.at[base + d],
                recvs.at[base + d],
                device,
            )
            copy.start()
            copies.append(copy)
        for copy in copies:
            copy.wait()
        means = [stats[base + d, pl.ds(0, 1), :] for d in range(axis_size)]
        mean = sum(means) / axis_size
        squares = sum(stats[base + d, pl.ds(1, 1), :] for d in range(axis_size))
        spread = sum((m - mean) * (m - mean) for m in means)
        return mean, squares + size * spread

    def norm(acc, n, gain, shift):
        own = jnp.broadcast_to(jnp.sum(acc, axis=1, keepdims=True) / cells, square)
        across = jnp.concatenate([own] * (width // LANES), axis=1)

        def body(phase, squares):
            for q in range(count):
                at = pl.ds(phase * depth + q * chans, chans)
                diff = held(at) - across
                squares = squares + fold(diff * diff)
            return squares

        squares = lax.fori_loop(0, phases, body, jnp.zeros(square, F32))
        squares = jnp.broadcast_to(jnp.sum(squares, axis=1, keepdims=True), square)
        mean, squares = merge(
            to_lanes(own), to_lanes(squares), cells, col_stats, cs_send, cs_recv, n, cols, False
        )
        mean, squares = merge(
            mean, squares, cells * cols, row_stats, rs_send, rs_recv, n, rows, True
        )
        factor = gain[...] * lax.rsqrt(squares / (cells * (rows * cols)) + EPSILON)
        repeat = lambda v: jnp.concatenate([to_rows(v)] * (width // LANES), axis=1)
        return repeat(mean), repeat(factor), repeat(shift[...])

    halo_start(pad_one, 0)
    band(0, first_ref)
    band(1, second_ref)
    halo_finish(pad_one, 0)
    mean, factor, shift = norm(conv(pad_one, 0), 0, gain_one, shift_one)

    def activate(phase, carry):
        for q in range(count):
            cell = held(pl.ds(phase * depth + q * chans, chans))
            cell = jnp.maximum((cell - mean) * factor + shift, 0.0)
            pad_two[phase, pl.ds((q + 1) * chans, chans), centre] = cell.astype(BF16)
        return carry

    lax.fori_loop(0, phases, activate, 0)
    halo_start(pad_two, 1)
    halo_finish(pad_two, 1)
    mean, factor, shift = norm(conv(pad_two, 1), 1, gain_two, shift_two)

    def finish(phase, carry):
        for q in range(count):
            at = pl.ds(phase * depth + q * chans, chans)
            cell = (held(at) - mean) * factor + shift
            cell = (x_ref[phase, pl.ds(q * chans, chans), :].astype(F32) + cell).astype(BF16)
            summed[phase, q] = cell
            keep(at, cell.astype(F32))
        return carry

    lax.fori_loop(0, phases, finish, 0)

    def direct(source_col, source_block):
        z, p = lax.rem(source_col, 4), lax.rem(source_block, 4)
        chosen = (z == p) & (lax.rem(source_col + source_block, 8) < 4)
        for a, b in DIRECT:
            chosen = chosen | ((z == a) & (p == b))
        return chosen

    mine = direct(col, block)

    def band_of(k):
        return pl.ds((k // phases) * PART, PART)

    def source(h, k):
        return summed.at[k % phases, :, band_of(k), pl.ds(h * height, height)]

    def landing(e, k):
        return got.at[k % phases, pl.ds(e * count, count), band_of(k), :]

    def waypoint(slot, k):
        return relay.at[slot, k % phases, :, band_of(k), :]

    def straight(h, k):
        return remote(
            source(h, k),
            landing(part, k),
            send.at[h * pieces + k],
            recv.at[part * pieces + k],
            (ratio * col + h, block),
        )

    def arrive(e, k):
        return remote(
            landing(e, k),
            landing(e, k),
            send.at[e * pieces + k],
            recv.at[e * pieces + k],
            (row, col),
        )

    def first_leg(h, k):
        slot = (lax.rem(block - col + cols, cols) - 1) * ratio + part
        return remote(
            source(h, k),
            waypoint(slot, k),
            send.at[h * pieces + k],
            relay_recv.at[slot * pieces + k],
            (ratio * col + h, col),
        )

    def second_leg(d, e, k):
        slot = (d - 1) * ratio + e
        return remote(
            waypoint(slot, k),
            landing(e, k),
            relay_send.at[slot * pieces + k],
            recv.at[e * pieces + k],
            (row, lax.rem(col + d, cols)),
        )

    @pl.when(jnp.logical_not(relays) & mine)
    def _():
        for k in range(pieces):
            for h in range(ratio):
                straight(h, k).start()

    @pl.when(jnp.logical_not(relays | mine))
    def _():
        for k in range(pieces):
            for h in range(ratio):
                first_leg(h, k).start()

    @pl.when(relays)
    def _():
        for h in range(ratio):

            @pl.when(part != h)
            def _(h=h):
                for k in range(pieces):
                    straight(h, k).start()

            @pl.when(part == h)
            def _(h=h):
                got[:, pl.ds(h * count, count), :, :] = summed[
                    :, :, :, pl.ds(h * height, height)
                ]

        for k in range(pieces):
            for d in range(1, cols):

                @pl.when(jnp.logical_not(direct(col, lax.rem(col + d, cols))))
                def _(d=d, k=k):
                    for e in range(ratio):
                        slot = (d - 1) * ratio + e
                        remote(
                            waypoint(slot, k),
                            waypoint(slot, k),
                            relay_send.at[slot * pieces + k],
                            relay_recv.at[slot * pieces + k],
                            (row, col),
                        ).wait_recv()
                        second_leg(d, e, k).start()

    span = ratio * depth
    for p in range(parts):
        for phase in range(phases):
            k = p * phases + phase
            for e in range(ratio):

                @pl.when(jnp.logical_not(relays & (part == e)))
                def _(e=e, k=k):
                    arrive(e, k).wait_recv()

            def unfold(q, carry, p=p, phase=phase):
                wide[pl.ds(phase * span + q * chans + p * PART, PART), :] = got[
                    phase, q, pl.ds(p * PART, PART), :
                ].astype(F32)
                return carry

            lax.fori_loop(0, ratio * count, unfold, 0, unroll=8)

        def turn(c, carry):
            own = jnp.concatenate(
                [
                    held(pl.ds(q * chans + c, phases, stride=depth))
                    for q in range(count)
                ],
                axis=0,
            )
            other = jnp.concatenate(
                [
                    wide[pl.ds(q * chans + c, phases, stride=span), :]
                    for q in range(ratio * count)
                ],
                axis=0,
            )
            total = own + jnp.swapaxes(other, 0, 1)
            out_ref[c] = (total * 0.5).astype(BF16)
            return carry

        lax.fori_loop(p * PART, (p + 1) * PART, turn, 0)

    for k in range(pieces):
        for h in range(ratio):

            @pl.when(jnp.logical_not(relays & (part == h)))
            def _(h=h, k=k):
                straight(h, k).wait_send()

    @pl.when(relays)
    def _():
        for k in range(pieces):
            for d in range(1, cols):

                @pl.when(jnp.logical_not(direct(col, lax.rem(col + d, cols))))
                def _(d=d, k=k):
                    for e in range(ratio):
                        second_leg(d, e, k).wait_send()


def run(rows, cols, features, first, second, scales):
    chans, height, width = features.shape
    count = height // STEP
    depth = count * chans
    ratio = rows // cols
    slots = (cols - 1) * ratio
    pieces = (chans // PART) * STEP
    full = depth + 2 * chans
    x = jnp.transpose(features.reshape(chans, count, STEP, width), (2, 1, 0, 3))
    x = x.reshape(STEP, depth, width)
    scales = [jnp.pad(v, (0, LANES - chans)).reshape(1, LANES) for v in scales]
    vmem = pl.BlockSpec(memory_space=pltpu.VMEM)
    dma = pltpu.SemaphoreType.DMA
    return pl.pallas_call(
        functools.partial(kernel, rows, cols),
        out_shape=jax.ShapeDtypeStruct(features.shape, BF16),
        in_specs=[vmem] * 7,
        out_specs=vmem,
        scratch_shapes=[
            pltpu.VMEM((STEP, full, width + 2 * LANES), BF16),
            pltpu.VMEM((STEP, full, width + 2 * LANES), BF16),
            pltpu.VMEM((width // LANES, STEP * depth, LANES), F32),
            pltpu.VMEM((2 * STEP, 2 * LANES, LANES), BF16),
            pltpu.VMEM((2 * STEP, LANES, 2 * LANES), BF16),
            pltpu.VMEM((2, 3, GROUP * chans, (GROUP + 2) * chans), BF16),
            pltpu.VMEM((2, 2, depth // 2, LANES), BF16),
            pltpu.VMEM((2, 2, depth // 2 + 2 * chans, LANES), BF16),
            pltpu.VMEM((2 * cols, 8, LANES), F32),
            pltpu.VMEM((2 * rows, 8, LANES), F32),
            pltpu.VMEM((STEP, count, chans, width), BF16),
            pltpu.VMEM((STEP, ratio * count, chans, height), BF16),
            pltpu.VMEM((STEP * ratio * depth, height), F32),
            pltpu.VMEM((slots, STEP, count, chans, height), BF16),
            dma((16,)),
            dma((16,)),
            dma((2 * cols,)),
            dma((2 * cols,)),
            dma((2 * rows,)),
            dma((2 * rows,)),
            dma((ratio * pieces,)),
            dma((ratio * pieces,)),
            dma((slots * pieces,)),
            dma((slots * pieces,)),
        ],
        compiler_params=pltpu.CompilerParams(
            collective_id=0, has_side_effects=True, vmem_limit_bytes=56 * 1024 * 1024
        ),
    )(x, first, second, *scales)


def solution(mesh):
    rows, cols = mesh.shape["row"], mesh.shape["col"]

    def per_device(features, first, second, gain_one, shift_one, gain_two, shift_two):
        scales = (gain_one, shift_one, gain_two, shift_two)
        return run(rows, cols, features, first, second, scales)

    placed = (P(None, "row", "col"), P(), P(), P(), P(), P(), P())
    return jax.shard_map(
        per_device, mesh=mesh, in_specs=placed, out_specs=P(None, "row", "col"), check_vma=False
    )
```

time: 131 us -> 112 us (0.85)
  Pallas kernels: 123 us -> 102 us
  local copies, waits for them, and re-layouts: 6.95 us -> 9.65 us
    pallas_call x2 -> x1, Pallas kernels: 123 us -> 102 us  [run(): pl.pallas_call(functools.partial(kernel, rows, cols), out_shape=jax.Shape...]
    reshape x6 -> x3, local copies, waits for them, and re-layouts: 3.72 us -> 6.52 us  [the longest x1 4.08 us: run(): x = jnp.transpose(features.reshape(chans, count, STEP, width), (2, 1, 0, 3))]
    unnamed x5 -> x1, local copies, waits for them, and re-layouts: 1.96 us -> 3.13 us
where the time goes in v1:
time: 112 us
  Pallas kernels  102 us (91%)
  local copies, waits for them, and re-layouts  9.65 us (9%)
    pallas_call x1, Pallas kernels, run(): pl.pallas_call(functools.partial(kernel, rows, cols), out_shape=jax.Shape...  102 us
    reshape x1, local copies, waits for them, and re-layouts, run(): x = jnp.transpose(features.reshape(chans, count, STEP, width), (2, 1, 0, 3))  4.08 us
    unnamed x1, local copies, waits for them, and re-layouts  3.13 us
    reshape x2, local copies, waits for them, and re-layouts, run(): scales = [jnp.pad(v, (0, LANES - chans)).reshape(1, LANES) for v in scales]  2.43 us

profile of v1, /device:TPU:1, one launch (start us, length us, event | category | flops | bytes accessed | tf_op | source)
XLA Modules:
  0.0 111.5 jit_solution(14708389041729870694)
XLA Ops:
  0.0 1.2 %pad_bitcast_fusion.2 = (f32[1,128]{1,0:T(1,128)}, f32[1,128]{1,0:T(1,128)}) fusion(f32[32]{0:T(128)} %param.11, f32[32]{0:T(128)} %param.10), kind=kLoop, calls=%fused_computation.2 | loop fusion | bytes 1280 | tf_op jit(solution)/shard_map/reshape | solution.py:512
  1.2 1.2 %pad_bitcast_fusion = (f32[1,128]{1,0:T(1,128)}, f32[1,128]{1,0:T(1,128)}) fusion(f32[32]{0:T(128)} %param.13, f32[32]{0:T(128)} %param.12), kind=kLoop, calls=%fused_computation | loop fusion | bytes 1280 | tf_op jit(solution)/shard_map/reshape | solution.py:512
  2.4 4.1 %copy.8 = bf16[32,16,8,256]{3,0,1,2:T(8,128)(2,1)} copy(bf16[32,16,8,256]{3,2,1,0:T(8,128)(2,1)} %bitcast.13) | data formatting | bytes 4194304 | tf_op jit(solution)/shard_map/reshape | solution.py:510
  6.5 101.9 %shard_map.73 = bf16[32,128,256]{2,1,0:T(8,128)(2,1)} custom-call(bf16[8,512,256]{2,1,0:T(8,128)(2,1)} %bitcast.12, bf16[3,3,32,32]{3,2,1,0:T(8,128)(2,1)} %first_ref.1, bf16[3,3,32,32]{3,2,1,0:T(8,128)(2,1)} %second_ref.1, f32[1,128]{1,0:T(1,128)} %get-tuple-element.8.gain_one, f32[1,128]{1,0:T(1,128)} %get-tuple-element.7.shift_one, ...), custom_call_target="tpu_custom_call" | custom-call | tf_op jit(solution)/shard_map/pallas_call | solution.py:515
  108.4 3.1 %copy.10 = bf16[32,128,256]{2,1,0:T(8,128)(2,1)} copy(bf16[32,128,256]{2,1,0:T(8,128)(2,1)} %shard_map.73) | data formatting | bytes 4194304

commit v2 on v1

--- a/solution.py
+++ b/solution.py
@@ -59,7 +59,6 @@
     pad_two,
     hidden,
     pack_sel,
-    unpack_sel,
     weights,
     packed,
     strips,
@@ -98,10 +97,12 @@
     pieces = parts * phases
 
     for pad in (pad_one, pad_two):
-        pad[:, pl.ds(0, chans), :] = jnp.zeros((phases, chans, width + 2 * LANES), BF16)
-        pad[:, pl.ds(depth + chans, chans), :] = jnp.zeros(
-            (phases, chans, width + 2 * LANES), BF16
-        )
+        for at, size in ((0, chans), (depth + chans, chans)):
+            pad[:, pl.ds(at, size), :] = jnp.zeros((phases, size, width + 2 * LANES), BF16)
+        for at in (0, width + LANES):
+            pad[:, pl.ds(chans, depth), pl.ds(at, LANES)] = jnp.zeros(
+                (phases, depth, LANES), BF16
+            )
     strips[...] = jnp.zeros_like(strips)
 
     barrier = pltpu.get_barrier_semaphore()
@@ -135,18 +136,14 @@
     pad_one[:, pl.ds(chans, depth), centre] = x_ref[...]
 
     i, j = iota((2 * LANES, LANES), 0), iota((2 * LANES, LANES), 1)
-    in_half, source_lane = i // LANES, i % LANES
     edge = LANES - STEP
+    lane = i % LANES
+    goal = (i // LANES) * half_lanes + lane - j
+    head = jnp.where(lane < STEP, goal, -LANES)
+    tail = jnp.where(lane >= edge, goal - edge, -LANES)
     for phase in range(phases):
-        at = in_half * half_lanes + phase * STEP
-        pack_sel[phase] = one_hot((source_lane < STEP) & (j == source_lane + at))
-        pack_sel[phases + phase] = one_hot((source_lane >= edge) & (j == source_lane - edge + at))
-    i, j = iota((LANES, 2 * LANES), 0), iota((LANES, 2 * LANES), 1)
-    in_half, target_lane = j // LANES, j % LANES
-    for phase in range(phases):
-        at = in_half * half_lanes + phase * STEP
-        unpack_sel[phase] = one_hot((target_lane >= edge) & (i == target_lane - edge + at))
-        unpack_sel[phases + phase] = one_hot((target_lane < STEP) & (i == target_lane + at))
+        pack_sel[phase] = one_hot(head == -phase * STEP)
+        pack_sel[phases + phase] = one_hot(tail == -phase * STEP)
 
     def band(n, kernel_ref):
         span = (GROUP + 2) * chans
@@ -209,19 +206,6 @@
                 back.wait_recv()
                 copy.wait_send()
 
-        for side, lane in ((0, 0), (1, width + LANES)):
-            at = pl.ds(lane, LANES)
-
-            def body(phase, carry, side=side, at=at):
-                placed = dot(strips[n, side], unpack_sel[side * phases + phase]).astype(BF16)
-                pad[phase, pl.ds(chans, fold_rows), at] = placed[:fold_rows, :LANES]
-                pad[phase, pl.ds(chans + fold_rows, fold_rows), at] = placed[:fold_rows, LANES:]
-                pad[phase, pl.ds(0, chans), at] = placed[fold_rows : fold_rows + chans, LANES:]
-                pad[phase, pl.ds(full - chans, chans), at] = placed[fold_rows + chans :, :LANES]
-                return carry
-
-            lax.fori_loop(0, phases, body, 0, unroll=4)
-
     tiles = width // LANES
 
     def held(at):
@@ -235,20 +219,57 @@
         total = jnp.sum(values.reshape(-1, chans, width), axis=0)
         return sum(total[:, k : k + LANES] for k in range(0, width, LANES))
 
+    def taps(pad, n, groups, acc):
+        def body(phase, acc):
+            for first, last in groups:
+                low = first * GROUP * chans
+                rows_in = ((last - first) * GROUP + 2) * chans
+                shifted = [
+                    pad[phase, pl.ds(low, rows_in), pl.ds(LANES + (b - 1) * STEP, width)]
+                    for b in range(3)
+                ]
+                for g in range(last - first):
+                    at = g * GROUP * chans
+                    result = sum(
+                        dot(weights[n, b], shifted[b][at : at + (GROUP + 2) * chans])
+                        for b in range(3)
+                    )
+                    keep(pl.ds(phase * depth + low + at, GROUP * chans), result)
+                    acc = acc + fold(result)
+            return acc
+
+        return lax.fori_loop(0, phases, body, acc, unroll=2)
+
+    def strip_taps(n, side, acc):
+        swap = lambda v: jnp.concatenate([v[:, half_lanes:], v[:, :half_lanes]], axis=1)
+        whole = strips[n, side, pl.ds(0, fold_rows), :]
+        up = strips[n, side, pl.ds(fold_rows, chans), :]
+        down = strips[n, side, pl.ds(fold_rows + chans, chans), :]
+        column = jnp.concatenate([swap(up), whole, swap(whole), down], axis=0)
+        lanes = iota((GROUP * chans, LANES), 1)
+        if side == 0:
+            tile, start, wanted = 0, 0, lanes < STEP
+        else:
+            tile, start, wanted = tiles - 1, edge, lanes >= edge
+        for g in range(count // GROUP):
+            low = g * GROUP * chans
+            added = dot(weights[n, 2 * side], column[low : low + (GROUP + 2) * chans])
+            added = jnp.where(lanes < half_lanes, added, 0.0)
+            acc = acc + jnp.sum(added.reshape(GROUP, chans, LANES), axis=0)
+            for phase in range(phases):
+                at = pl.ds(phase * depth + low, GROUP * chans)
+                moved = pltpu.roll(added, (start - phase * STEP) % LANES, 1)
+                hidden[tile, at, :] = hidden[tile, at, :] + jnp.where(wanted, moved, 0.0)
+        return acc
+
     def conv(pad, n):
-        def body(phase, acc):
-            shifted = [
-                pad[phase, :, pl.ds(LANES + (b - 1) * STEP, width)] for b in range(3)
-            ]
-            for g in range(count // GROUP):
-                low = g * GROUP * chans
-                high = low + (GROUP + 2) * chans
-                result = sum(dot(weights[n, b], shifted[b][low:high]) for b in range(3))
-                keep(pl.ds(phase * depth + low, GROUP * chans), result)
-                acc = acc + fold(result)
-            return acc
-
-        return lax.fori_loop(0, phases, body, jnp.zeros((chans, LANES), F32), unroll=2)
+        last = count // GROUP
+        acc = taps(pad, n, ((1, last - 1),), jnp.zeros((chans, LANES), F32))
+        halo_finish(pad, n)
+        acc = taps(pad, n, ((0, 1), (last - 1, last)), acc)
+        for side in range(2):
+            acc = strip_taps(n, side, acc)
+        return acc
 
     square = (chans, LANES)
     diagonal = iota(square, 0) == iota(square, 1)
@@ -299,7 +320,7 @@
                 squares = squares + fold(diff * diff)
             return squares
 
-        squares = lax.fori_loop(0, phases, body, jnp.zeros(square, F32))
+        squares = lax.fori_loop(0, phases, body, jnp.zeros(square, F32), unroll=2)
         squares = jnp.broadcast_to(jnp.sum(squares, axis=1, keepdims=True), square)
         mean, squares = merge(
             to_lanes(own), to_lanes(squares), cells, col_stats, cs_send, cs_recv, n, cols, False
@@ -307,14 +328,16 @@
         mean, squares = merge(
             mean, squares, cells * cols, row_stats, rs_send, rs_recv, n, rows, True
         )
-        factor = gain[...] * lax.rsqrt(squares / (cells * (rows * cols)) + EPSILON)
+        blank = jnp.zeros((1, LANES - chans), F32)
+        gains = jnp.concatenate([gain[...], blank], axis=1)
+        shifts = jnp.concatenate([shift[...], blank], axis=1)
+        factor = gains * lax.rsqrt(squares / (cells * (rows * cols)) + EPSILON)
         repeat = lambda v: jnp.concatenate([to_rows(v)] * (width // LANES), axis=1)
-        return repeat(mean), repeat(factor), repeat(shift[...])
+        return repeat(mean), repeat(factor), repeat(shifts)
 
     halo_start(pad_one, 0)
     band(0, first_ref)
     band(1, second_ref)
-    halo_finish(pad_one, 0)
     mean, factor, shift = norm(conv(pad_one, 0), 0, gain_one, shift_one)
 
     def activate(phase, carry):
@@ -326,19 +349,7 @@
 
     lax.fori_loop(0, phases, activate, 0)
     halo_start(pad_two, 1)
-    halo_finish(pad_two, 1)
     mean, factor, shift = norm(conv(pad_two, 1), 1, gain_two, shift_two)
-
-    def finish(phase, carry):
-        for q in range(count):
-            at = pl.ds(phase * depth + q * chans, chans)
-            cell = (held(at) - mean) * factor + shift
-            cell = (x_ref[phase, pl.ds(q * chans, chans), :].astype(F32) + cell).astype(BF16)
-            summed[phase, q] = cell
-            keep(at, cell.astype(F32))
-        return carry
-
-    lax.fori_loop(0, phases, finish, 0)
 
     def direct(source_col, source_block):
         z, p = lax.rem(source_col, 4), lax.rem(source_block, 4)
@@ -350,7 +361,7 @@
     mine = direct(col, block)
 
     def band_of(k):
-        return pl.ds((k // phases) * PART, PART)
+        return pl.ds(pl.multiple_of((k // phases) * PART, PART), PART)
 
     def source(h, k):
         return summed.at[k % phases, :, band_of(k), pl.ds(h * height, height)]
@@ -399,26 +410,40 @@
             (row, lax.rem(col + d, cols)),
         )
 
-    @pl.when(jnp.logical_not(relays) & mine)
-    def _():
-        for k in range(pieces):
-            for h in range(ratio):
+    def issue(k):
+        goes = relays | mine | (k == pieces - 1)
+        for h in range(ratio):
+            here = relays & (part == h)
+
+            @pl.when(goes & jnp.logical_not(here))
+            def _(h=h):
                 straight(h, k).start()
 
-    @pl.when(jnp.logical_not(relays | mine))
-    def _():
-        for k in range(pieces):
-            for h in range(ratio):
+            @pl.when(jnp.logical_not(goes))
+            def _(h=h):
                 first_leg(h, k).start()
+
+    def finish(phase, carry):
+        for q in range(count):
+            at = pl.ds(phase * depth + q * chans, chans)
+            cell = (held(at) - mean) * factor + shift
+            cell = (x_ref[phase, pl.ds(q * chans, chans), :].astype(F32) + cell).astype(BF16)
+            summed[phase, q] = cell
+            keep(at, cell.astype(F32))
+        issue(phase)
+        return carry
+
+    lax.fori_loop(0, phases, finish, 0)
+
+    def issue_rest(k, carry):
+        issue(k)
+        return carry
+
+    lax.fori_loop(phases, pieces, issue_rest, 0)
 
     @pl.when(relays)
     def _():
         for h in range(ratio):
-
-            @pl.when(part != h)
-            def _(h=h):
-                for k in range(pieces):
-                    straight(h, k).start()
 
             @pl.when(part == h)
             def _(h=h):
@@ -426,11 +451,11 @@
                     :, :, :, pl.ds(h * height, height)
                 ]
 
-        for k in range(pieces):
+        def forward(k, carry):
             for d in range(1, cols):
 
                 @pl.when(jnp.logical_not(direct(col, lax.rem(col + d, cols))))
-                def _(d=d, k=k):
+                def _(d=d):
                     for e in range(ratio):
                         slot = (d - 1) * ratio + e
                         remote(
@@ -442,23 +467,27 @@
                         ).wait_recv()
                         second_leg(d, e, k).start()
 
+            return carry
+
+        lax.fori_loop(0, pieces - 1, forward, 0)
+
     span = ratio * depth
     for p in range(parts):
-        for phase in range(phases):
+        def collect(phase, carry, p=p):
             k = p * phases + phase
             for e in range(ratio):
 
                 @pl.when(jnp.logical_not(relays & (part == e)))
-                def _(e=e, k=k):
+                def _(e=e):
                     arrive(e, k).wait_recv()
 
-            def unfold(q, carry, p=p, phase=phase):
+            for q in range(ratio * count):
                 wide[pl.ds(phase * span + q * chans + p * PART, PART), :] = got[
                     phase, q, pl.ds(p * PART, PART), :
                 ].astype(F32)
-                return carry
-
-            lax.fori_loop(0, ratio * count, unfold, 0, unroll=8)
+            return carry
+
+        lax.fori_loop(0, phases, collect, 0)
 
         def turn(c, carry):
             own = jnp.concatenate(
@@ -479,24 +508,32 @@
             out_ref[c] = (total * 0.5).astype(BF16)
             return carry
 
-        lax.fori_loop(p * PART, (p + 1) * PART, turn, 0)
-
-    for k in range(pieces):
+        lax.fori_loop(p * PART, (p + 1) * PART, turn, 0, unroll=4)
+
+    def drain(k, carry):
         for h in range(ratio):
 
             @pl.when(jnp.logical_not(relays & (part == h)))
-            def _(h=h, k=k):
+            def _(h=h):
                 straight(h, k).wait_send()
+
+        return carry
+
+    lax.fori_loop(0, pieces, drain, 0)
 
     @pl.when(relays)
     def _():
-        for k in range(pieces):
+        def drain_relay(k, carry):
             for d in range(1, cols):
 
                 @pl.when(jnp.logical_not(direct(col, lax.rem(col + d, cols))))
-                def _(d=d, k=k):
+                def _(d=d):
                     for e in range(ratio):
                         second_leg(d, e, k).wait_send()
+
+            return carry
+
+        lax.fori_loop(0, pieces - 1, drain_relay, 0)
 
 
 def run(rows, cols, features, first, second, scales):
@@ -509,7 +546,7 @@
     full = depth + 2 * chans
     x = jnp.transpose(features.reshape(chans, count, STEP, width), (2, 1, 0, 3))
     x = x.reshape(STEP, depth, width)
-    scales = [jnp.pad(v, (0, LANES - chans)).reshape(1, LANES) for v in scales]
+    scales = [v.reshape(1, chans) for v in scales]
     vmem = pl.BlockSpec(memory_space=pltpu.VMEM)
     dma = pltpu.SemaphoreType.DMA
     return pl.pallas_call(
@@ -522,7 +559,6 @@
             pltpu.VMEM((STEP, full, width + 2 * LANES), BF16),
             pltpu.VMEM((width // LANES, STEP * depth, LANES), F32),
             pltpu.VMEM((2 * STEP, 2 * LANES, LANES), BF16),
-            pltpu.VMEM((2 * STEP, LANES, 2 * LANES), BF16),
             pltpu.VMEM((2, 3, GROUP * chans, (GROUP + 2) * chans), BF16),
             pltpu.VMEM((2, 2, depth // 2, LANES), BF16),
             pltpu.VMEM((2, 2, depth // 2 + 2 * chans, LANES), BF16),
@@ -544,7 +580,7 @@
             dma((slots * pieces,)),
         ],
         compiler_params=pltpu.CompilerParams(
-            collective_id=0, has_side_effects=True, vmem_limit_bytes=56 * 1024 * 1024
+            collective_id=0, has_side_effects=True, vmem_limit_bytes=44 * 1024 * 1024
         ),
     )(x, first, second, *scales)
 

time: 112 us -> 101 us (0.902)
  the two profiles are of different devices: /device:TPU:1 before, /device:TPU:3 now
where the time goes in v2:
time: 101 us
  Pallas kernels  96.4 us (95%)
  local copies, waits for them, and re-layouts  4.2 us (4%)
    pallas_call x1, Pallas kernels, run(): pl.pallas_call(functools.partial(kernel, rows, cols), out_shape=jax.Shape...  96.4 us
    reshape x1, local copies, waits for them, and re-layouts, run(): x = jnp.transpose(features.reshape(chans, count, STEP, width), (2, 1, 0, 3))  2.86 us

profile of v2, /device:TPU:3, one launch (start us, length us, event | category | flops | bytes accessed | tf_op | source)
XLA Modules:
  0.0 100.7 jit_solution(14853515471912102487)
XLA Ops:
  0.0 0.0 copy-start
  0.0 0.0 copy-start.1
  0.0 0.0 copy-start.2
  0.0 0.0 copy-start.3
  0.0 0.0 copy-start.4
  0.0 0.0 copy-start.5
  0.0 2.9 %copy.8 = bf16[32,16,8,256]{3,0,1,2:T(8,128)(2,1)S(1)} copy(bf16[32,16,8,256]{3,2,1,0:T(8,128)(2,1)} %bitcast.13) | data formatting | bytes 4194304 | tf_op jit(solution)/shard_map/reshape | solution.py:547
  2.9 0.0 copy-done
  2.9 0.0 copy-done.1
  2.9 0.0 copy-done.2
  2.9 0.0 copy-done.3
  2.9 0.0 copy-done.4
  3.0 0.0 copy-done.5
  3.0 96.4 %shard_map.73 = bf16[32,128,256]{2,1,0:T(8,128)(2,1)S(1)} custom-call(bf16[8,512,256]{2,1,0:T(8,128)(2,1)S(1)} %bitcast.8, bf16[3,3,32,32]{3,2,1,0:T(8,128)(2,1)S(1)} %copy-done, bf16[3,3,32,32]{3,2,1,0:T(8,128)(2,1)S(1)} %copy-done.1, f32[1,32]{1,0:T(1,128)S(1)} %bitcast.9, f32[1,32]{1,0:T(1,128)S(1)} %bitcast.10, f32[1,32]{1,0:T(1,128)S(1)} %bitcast.11, ...), custom_call_target="tpu_custom_call" | custom-call | tf_op jit(solution)/shard_map/pallas_call | solution.py:552
  99.4 1.3 %copy.10 = bf16[32,128,256]{2,1,0:T(8,128)(2,1)} copy(bf16[32,128,256]{2,1,0:T(8,128)(2,1)S(1)} %shard_map.73) | data formatting | bytes 4194304
Async XLA Ops:
  0.0 2.9 %copy-start = (bf16[3,3,32,32]{3,2,1,0:T(8,128)(2,1)S(1)}, bf16[3,3,32,32]{3,2,1,0:T(8,128)(2,1)}, u32[]{:S(2)}) copy-start(bf16[3,3,32,32]{3,2,1,0:T(8,128)(2,1)} %first_ref.1) | copy-start | bytes 55300
  0.0 2.9 %copy-start.1 = (bf16[3,3,32,32]{3,2,1,0:T(8,128)(2,1)S(1)}, bf16[3,3,32,32]{3,2,1,0:T(8,128)(2,1)}, u32[]{:S(2)}) copy-start(bf16[3,3,32,32]{3,2,1,0:T(8,128)(2,1)} %second_ref.1) | copy-start | bytes 55300
  0.0 2.9 %copy-start.2 = (f32[32]{0:T(128)S(1)}, f32[32]{0:T(128)}, u32[]{:S(2)}) copy-start(f32[32]{0:T(128)} %param.10) | copy-start | bytes 388
  0.0 2.9 %copy-start.3 = (f32[32]{0:T(128)S(1)}, f32[32]{0:T(128)}, u32[]{:S(2)}) copy-start(f32[32]{0:T(128)} %param.11) | copy-start | bytes 388
  0.0 2.9 %copy-start.4 = (f32[32]{0:T(128)S(1)}, f32[32]{0:T(128)}, u32[]{:S(2)}) copy-start(f32[32]{0:T(128)} %param.12) | copy-start | bytes 388
  0.0 2.9 %copy-start.5 = (f32[32]{0:T(128)S(1)}, f32[32]{0:T(128)}, u32[]{:S(2)}) copy-start(f32[32]{0:T(128)} %param.13) | copy-start | bytes 388

commit v3 on v2

--- a/solution.py
+++ b/solution.py
@@ -59,6 +59,7 @@
     pad_two,
     hidden,
     pack_sel,
+    edges,
     weights,
     packed,
     strips,
@@ -88,7 +89,6 @@
     fold_rows = depth // 2
     half_lanes = LANES // 2
     cells = float(phases * count * width)
-    centre = pl.ds(LANES, width)
     ratio = rows // cols
     block = lax.div(row, ratio)
     part = lax.rem(row, ratio)
@@ -98,11 +98,7 @@
 
     for pad in (pad_one, pad_two):
         for at, size in ((0, chans), (depth + chans, chans)):
-            pad[:, pl.ds(at, size), :] = jnp.zeros((phases, size, width + 2 * LANES), BF16)
-        for at in (0, width + LANES):
-            pad[:, pl.ds(chans, depth), pl.ds(at, LANES)] = jnp.zeros(
-                (phases, depth, LANES), BF16
-            )
+            pad[:, pl.ds(at, size), :] = jnp.zeros((phases, size, width), BF16)
     strips[...] = jnp.zeros_like(strips)
 
     barrier = pltpu.get_barrier_semaphore()
@@ -133,7 +129,7 @@
         pl.when(jnp.logical_not(relays))(functools.partial(greet, (ratio * col + h, block)))
     expected = expected + jnp.where(relays, 0, ratio)
 
-    pad_one[:, pl.ds(chans, depth), centre] = x_ref[...]
+    pad_one[:, pl.ds(chans, depth), :] = x_ref[...]
 
     i, j = iota((2 * LANES, LANES), 0), iota((2 * LANES, LANES), 1)
     edge = LANES - STEP
@@ -163,8 +159,8 @@
         if dc == 0:
             source = chans if dr < 0 else depth
             target = depth + chans if dr < 0 else 0
-            src = pad.at[:, pl.ds(source, chans), centre]
-            dst = pad.at[:, pl.ds(target, chans), centre]
+            src = pad.at[:, pl.ds(source, chans)]
+            dst = pad.at[:, pl.ds(target, chans)]
         else:
             mine, theirs = (0, 1) if dc < 0 else (1, 0)
             if dr == 0:
@@ -183,7 +179,7 @@
         for k in (1, 6):
             there, copy = halo_copy(pad, n, k)
             pl.when(there)(copy.start)
-        for side, lane in ((0, LANES), (1, width)):
+        for side, lane in ((0, 0), (1, width - LANES)):
             total = jnp.zeros((fold_rows, LANES), F32)
             for phase in range(phases):
                 low = pad[phase, pl.ds(chans, fold_rows), pl.ds(lane, LANES)]
@@ -224,10 +220,13 @@
             for first, last in groups:
                 low = first * GROUP * chans
                 rows_in = ((last - first) * GROUP + 2) * chans
-                shifted = [
-                    pad[phase, pl.ds(low, rows_in), pl.ds(LANES + (b - 1) * STEP, width)]
-                    for b in range(3)
-                ]
+                middle = pad[phase, pl.ds(low, rows_in), :]
+                blank = jnp.zeros((rows_in, STEP), BF16)
+                shifted = (
+                    jnp.concatenate([blank, middle[:, : width - STEP]], axis=1),
+                    middle,
+                    jnp.concatenate([middle[:, STEP:], blank], axis=1),
+                )
                 for g in range(last - first):
                     at = g * GROUP * chans
                     result = sum(
@@ -238,7 +237,9 @@
                     acc = acc + fold(result)
             return acc
 
-        return lax.fori_loop(0, phases, body, acc, unroll=2)
+        return lax.fori_loop(0, phases, body, acc, unroll=True)
+
+    lanes = iota((GROUP * chans, LANES), 1)
 
     def strip_taps(n, side, acc):
         swap = lambda v: jnp.concatenate([v[:, half_lanes:], v[:, :half_lanes]], axis=1)
@@ -246,20 +247,12 @@
         up = strips[n, side, pl.ds(fold_rows, chans), :]
         down = strips[n, side, pl.ds(fold_rows + chans, chans), :]
         column = jnp.concatenate([swap(up), whole, swap(whole), down], axis=0)
-        lanes = iota((GROUP * chans, LANES), 1)
-        if side == 0:
-            tile, start, wanted = 0, 0, lanes < STEP
-        else:
-            tile, start, wanted = tiles - 1, edge, lanes >= edge
         for g in range(count // GROUP):
             low = g * GROUP * chans
             added = dot(weights[n, 2 * side], column[low : low + (GROUP + 2) * chans])
             added = jnp.where(lanes < half_lanes, added, 0.0)
+            edges[side, pl.ds(low, GROUP * chans), :] = added
             acc = acc + jnp.sum(added.reshape(GROUP, chans, LANES), axis=0)
-            for phase in range(phases):
-                at = pl.ds(phase * depth + low, GROUP * chans)
-                moved = pltpu.roll(added, (start - phase * STEP) % LANES, 1)
-                hidden[tile, at, :] = hidden[tile, at, :] + jnp.where(wanted, moved, 0.0)
         return acc
 
     def conv(pad, n):
@@ -311,16 +304,27 @@
 
     def norm(acc, n, gain, shift):
         own = jnp.broadcast_to(jnp.sum(acc, axis=1, keepdims=True) / cells, square)
-        across = jnp.concatenate([own] * (width // LANES), axis=1)
-
-        def body(phase, squares):
-            for q in range(count):
-                at = pl.ds(phase * depth + q * chans, chans)
-                diff = held(at) - across
-                squares = squares + fold(diff * diff)
-            return squares
-
-        squares = lax.fori_loop(0, phases, body, jnp.zeros(square, F32), unroll=2)
+        across = jnp.concatenate([own] * GROUP, axis=0)
+        squares = jnp.zeros(square, F32)
+        for phase in range(phases):
+            for g in range(count // GROUP):
+                low = g * GROUP * chans
+                at = pl.ds(phase * depth + low, GROUP * chans)
+                for k in range(tiles):
+                    cell = hidden[k, at, :]
+                    for side, tile, start in ((0, 0, 0), (1, tiles - 1, edge)):
+                        if k == tile:
+                            moved = pltpu.roll(
+                                edges[side, pl.ds(low, GROUP * chans), :],
+                                (start - phase * STEP) % LANES,
+                                1,
+                            )
+                            wanted = lanes >= edge if side else lanes < STEP
+                            cell = cell + jnp.where(wanted, moved, 0.0)
+                            hidden[k, at, :] = cell
+                    diff = cell - across
+                    diff = (diff * diff).reshape(GROUP, chans, LANES)
+                    squares = squares + jnp.sum(diff, axis=0)
         squares = jnp.broadcast_to(jnp.sum(squares, axis=1, keepdims=True), square)
         mean, squares = merge(
             to_lanes(own), to_lanes(squares), cells, col_stats, cs_send, cs_recv, n, cols, False
@@ -344,7 +348,7 @@
         for q in range(count):
             cell = held(pl.ds(phase * depth + q * chans, chans))
             cell = jnp.maximum((cell - mean) * factor + shift, 0.0)
-            pad_two[phase, pl.ds((q + 1) * chans, chans), centre] = cell.astype(BF16)
+            pad_two[phase, pl.ds((q + 1) * chans, chans), :] = cell.astype(BF16)
         return carry
 
     lax.fori_loop(0, phases, activate, 0)
@@ -555,10 +559,11 @@
         in_specs=[vmem] * 7,
         out_specs=vmem,
         scratch_shapes=[
-            pltpu.VMEM((STEP, full, width + 2 * LANES), BF16),
-            pltpu.VMEM((STEP, full, width + 2 * LANES), BF16),
+            pltpu.VMEM((STEP, full, width), BF16),
+            pltpu.VMEM((STEP, full, width), BF16),
             pltpu.VMEM((width // LANES, STEP * depth, LANES), F32),
             pltpu.VMEM((2 * STEP, 2 * LANES, LANES), BF16),
+            pltpu.VMEM((2, depth, LANES), F32),
             pltpu.VMEM((2, 3, GROUP * chans, (GROUP + 2) * chans), BF16),
             pltpu.VMEM((2, 2, depth // 2, LANES), BF16),
             pltpu.VMEM((2, 2, depth // 2 + 2 * chans, LANES), BF16),

time: 101 us -> 96.2 us (0.952)
  Pallas kernels: 96.4 us -> 91.8 us
    pallas_call x1, Pallas kernels: 96.4 us -> 91.8 us  [run(): pl.pallas_call(functools.partial(kernel, rows, cols), out_shape=jax.Shape...]
where the time goes in v3:
time: 96.2 us; the launch traced here: 96.1 us
  Pallas kernels  91.8 us (95%)
  local copies, waits for them, and re-layouts  4.2 us (4%)
    pallas_call x1, Pallas kernels, run(): pl.pallas_call(functools.partial(kernel, rows, cols), out_shape=jax.Shape...  91.8 us
    reshape x1, local copies, waits for them, and re-layouts, run(): x = jnp.transpose(features.reshape(chans, count, STEP, width), (2, 1, 0, 3))  2.86 us

profile of v3, /device:TPU:3, one launch (start us, length us, event | category | flops | bytes accessed | tf_op | source)
XLA Modules:
  0.0 96.1 jit_solution(17675275496191026212)
XLA Ops:
  0.0 0.0 copy-start
  0.0 0.0 copy-start.1
  0.0 0.0 copy-start.2
  0.0 0.0 copy-start.3
  0.0 0.0 copy-start.4
  0.0 0.0 copy-start.5
  0.0 2.9 %copy.8 = bf16[32,16,8,256]{3,0,1,2:T(8,128)(2,1)S(1)} copy(bf16[32,16,8,256]{3,2,1,0:T(8,128)(2,1)} %bitcast.13) | data formatting | bytes 4194304 | tf_op jit(solution)/shard_map/reshape | solution.py:551
  2.9 0.0 copy-done
  2.9 0.0 copy-done.1
  2.9 0.0 copy-done.2
  2.9 0.0 copy-done.3
  2.9 0.0 copy-done.4
  3.0 0.0 copy-done.5
  3.0 91.8 %shard_map.73 = bf16[32,128,256]{2,1,0:T(8,128)(2,1)S(1)} custom-call(bf16[8,512,256]{2,1,0:T(8,128)(2,1)S(1)} %bitcast.8, bf16[3,3,32,32]{3,2,1,0:T(8,128)(2,1)S(1)} %copy-done, bf16[3,3,32,32]{3,2,1,0:T(8,128)(2,1)S(1)} %copy-done.1, f32[1,32]{1,0:T(1,128)S(1)} %bitcast.9, f32[1,32]{1,0:T(1,128)S(1)} %bitcast.10, f32[1,32]{1,0:T(1,128)S(1)} %bitcast.11, ...), custom_call_target="tpu_custom_call" | custom-call | tf_op jit(solution)/shard_map/pallas_call | solution.py:556
  94.8 1.3 %copy.10 = bf16[32,128,256]{2,1,0:T(8,128)(2,1)} copy(bf16[32,128,256]{2,1,0:T(8,128)(2,1)S(1)} %shard_map.73) | data formatting | bytes 4194304
Async XLA Ops:
  0.0 2.9 %copy-start = (bf16[3,3,32,32]{3,2,1,0:T(8,128)(2,1)S(1)}, bf16[3,3,32,32]{3,2,1,0:T(8,128)(2,1)}, u32[]{:S(2)}) copy-start(bf16[3,3,32,32]{3,2,1,0:T(8,128)(2,1)} %first_ref.1) | copy-start | bytes 55300
  0.0 2.9 %copy-start.1 = (bf16[3,3,32,32]{3,2,1,0:T(8,128)(2,1)S(1)}, bf16[3,3,32,32]{3,2,1,0:T(8,128)(2,1)}, u32[]{:S(2)}) copy-start(bf16[3,3,32,32]{3,2,1,0:T(8,128)(2,1)} %second_ref.1) | copy-start | bytes 55300
  0.0 2.9 %copy-start.2 = (f32[32]{0:T(128)S(1)}, f32[32]{0:T(128)}, u32[]{:S(2)}) copy-start(f32[32]{0:T(128)} %param.10) | copy-start | bytes 388
  0.0 2.9 %copy-start.3 = (f32[32]{0:T(128)S(1)}, f32[32]{0:T(128)}, u32[]{:S(2)}) copy-start(f32[32]{0:T(128)} %param.11) | copy-start | bytes 388
  0.0 2.9 %copy-start.4 = (f32[32]{0:T(128)S(1)}, f32[32]{0:T(128)}, u32[]{:S(2)}) copy-start(f32[32]{0:T(128)} %param.12) | copy-start | bytes 388
  0.0 2.9 %copy-start.5 = (f32[32]{0:T(128)S(1)}, f32[32]{0:T(128)}, u32[]{:S(2)}) copy-start(f32[32]{0:T(128)} %param.13) | copy-start | bytes 388

commit v4 on v3

--- a/solution.py
+++ b/solution.py
@@ -364,6 +364,14 @@
 
     mine = direct(col, block)
 
+    def crosses(target):
+        return (2 * col < cols) != (2 * target < cols)
+
+    def passes(d, k):
+        target = lax.rem(col + d, cols)
+        straight_on = (k == pieces - 1) & crosses(target)
+        return jnp.logical_not(direct(col, target) | straight_on)
+
     def band_of(k):
         return pl.ds(pl.multiple_of((k // phases) * PART, PART), PART)
 
@@ -415,7 +423,7 @@
         )
 
     def issue(k):
-        goes = relays | mine | (k == pieces - 1)
+        goes = relays | mine | ((k == pieces - 1) & crosses(block))
         for h in range(ratio):
             here = relays & (part == h)
 
@@ -455,28 +463,32 @@
                     :, :, :, pl.ds(h * height, height)
                 ]
 
-        def forward(k, carry):
-            for d in range(1, cols):
-
-                @pl.when(jnp.logical_not(direct(col, lax.rem(col + d, cols))))
-                def _(d=d):
-                    for e in range(ratio):
-                        slot = (d - 1) * ratio + e
-                        remote(
-                            waypoint(slot, k),
-                            waypoint(slot, k),
-                            relay_send.at[slot * pieces + k],
-                            relay_recv.at[slot * pieces + k],
-                            (row, col),
-                        ).wait_recv()
-                        second_leg(d, e, k).start()
-
-            return carry
-
-        lax.fori_loop(0, pieces - 1, forward, 0)
+    def forward(k, carry):
+        for d in range(1, cols):
+
+            @pl.when(passes(d, k))
+            def _(d=d):
+                for e in range(ratio):
+                    slot = (d - 1) * ratio + e
+                    remote(
+                        waypoint(slot, k),
+                        waypoint(slot, k),
+                        relay_send.at[slot * pieces + k],
+                        relay_recv.at[slot * pieces + k],
+                        (row, col),
+                    ).wait_recv()
+                    second_leg(d, e, k).start()
+
+        return carry
 
     span = ratio * depth
+    unit = one_hot(iota((height, height), 0) == iota((height, height), 1))
     for p in range(parts):
+
+        @pl.when(relays)
+        def _(p=p):
+            lax.fori_loop(p * phases, (p + 1) * phases, forward, 0)
+
         def collect(phase, carry, p=p):
             k = p * phases + phase
             for e in range(ratio):
@@ -508,7 +520,9 @@
                 ],
                 axis=0,
             )
-            total = own + jnp.swapaxes(other, 0, 1)
+            total = own + lax.dot_general(
+                unit, other.astype(BF16), (((1,), (1,)), ((), ())), preferred_element_type=F32
+            )
             out_ref[c] = (total * 0.5).astype(BF16)
             return carry
 
@@ -530,14 +544,14 @@
         def drain_relay(k, carry):
             for d in range(1, cols):
 
-                @pl.when(jnp.logical_not(direct(col, lax.rem(col + d, cols))))
+                @pl.when(passes(d, k))
                 def _(d=d):
                     for e in range(ratio):
                         second_leg(d, e, k).wait_send()
 
             return carry
 
-        lax.fori_loop(0, pieces - 1, drain_relay, 0)
+        lax.fori_loop(0, pieces, drain_relay, 0)
 
 
 def run(rows, cols, features, first, second, scales):

time: 96.2 us -> 93.7 us (0.974)
  Pallas kernels: 91.8 us -> 89 us
    pallas_call x1, Pallas kernels: 91.8 us -> 89 us  [run(): pl.pallas_call(functools.partial(kernel, rows, cols), out_shape=jax.Shape...]
where the time goes in v4:
time: 93.7 us; the launch traced here: 93.3 us
  Pallas kernels  89 us (95%)
  local copies, waits for them, and re-layouts  4.2 us (4%)
    pallas_call x1, Pallas kernels, run(): pl.pallas_call(functools.partial(kernel, rows, cols), out_shape=jax.Shape...  89 us
    reshape x1, local copies, waits for them, and re-layouts, run(): x = jnp.transpose(features.reshape(chans, count, STEP, width), (2, 1, 0, 3))  2.86 us

profile of v4, /device:TPU:3, one launch (start us, length us, event | category | flops | bytes accessed | tf_op | source)
XLA Modules:
  0.0 93.3 jit_solution(17053795961556922294)
XLA Ops:
  0.0 0.0 copy-start
  0.0 0.0 copy-start.1
  0.0 0.0 copy-start.2
  0.0 0.0 copy-start.3
  0.0 0.0 copy-start.4
  0.0 0.0 copy-start.5
  0.0 2.9 %copy.8 = bf16[32,16,8,256]{3,0,1,2:T(8,128)(2,1)S(1)} copy(bf16[32,16,8,256]{3,2,1,0:T(8,128)(2,1)} %bitcast.13) | data formatting | bytes 4194304 | tf_op jit(solution)/shard_map/reshape | solution.py:565
  2.9 0.0 copy-done
  2.9 0.0 copy-done.1
  2.9 0.0 copy-done.2
  2.9 0.0 copy-done.3
  2.9 0.0 copy-done.4
  3.0 0.0 copy-done.5
  3.0 89.0 %shard_map.73 = bf16[32,128,256]{2,1,0:T(8,128)(2,1)S(1)} custom-call(bf16[8,512,256]{2,1,0:T(8,128)(2,1)S(1)} %bitcast.8, bf16[3,3,32,32]{3,2,1,0:T(8,128)(2,1)S(1)} %copy-done, bf16[3,3,32,32]{3,2,1,0:T(8,128)(2,1)S(1)} %copy-done.1, f32[1,32]{1,0:T(1,128)S(1)} %bitcast.9, f32[1,32]{1,0:T(1,128)S(1)} %bitcast.10, f32[1,32]{1,0:T(1,128)S(1)} %bitcast.11, ...), custom_call_target="tpu_custom_call" | custom-call | tf_op jit(solution)/shard_map/pallas_call | solution.py:570
  92.0 1.3 %copy.10 = bf16[32,128,256]{2,1,0:T(8,128)(2,1)} copy(bf16[32,128,256]{2,1,0:T(8,128)(2,1)S(1)} %shard_map.73) | data formatting | bytes 4194304
Async XLA Ops:
  0.0 2.9 %copy-start = (bf16[3,3,32,32]{3,2,1,0:T(8,128)(2,1)S(1)}, bf16[3,3,32,32]{3,2,1,0:T(8,128)(2,1)}, u32[]{:S(2)}) copy-start(bf16[3,3,32,32]{3,2,1,0:T(8,128)(2,1)} %first_ref.1) | copy-start | bytes 55300
  0.0 2.9 %copy-start.1 = (bf16[3,3,32,32]{3,2,1,0:T(8,128)(2,1)S(1)}, bf16[3,3,32,32]{3,2,1,0:T(8,128)(2,1)}, u32[]{:S(2)}) copy-start(bf16[3,3,32,32]{3,2,1,0:T(8,128)(2,1)} %second_ref.1) | copy-start | bytes 55300
  0.0 2.9 %copy-start.2 = (f32[32]{0:T(128)S(1)}, f32[32]{0:T(128)}, u32[]{:S(2)}) copy-start(f32[32]{0:T(128)} %param.10) | copy-start | bytes 388
  0.0 2.9 %copy-start.3 = (f32[32]{0:T(128)S(1)}, f32[32]{0:T(128)}, u32[]{:S(2)}) copy-start(f32[32]{0:T(128)} %param.11) | copy-start | bytes 388
  0.0 2.9 %copy-start.4 = (f32[32]{0:T(128)S(1)}, f32[32]{0:T(128)}, u32[]{:S(2)}) copy-start(f32[32]{0:T(128)} %param.12) | copy-start | bytes 388
  0.0 2.9 %copy-start.5 = (f32[32]{0:T(128)S(1)}, f32[32]{0:T(128)}, u32[]{:S(2)}) copy-start(f32[32]{0:T(128)} %param.13) | copy-start | bytes 388

commit v5 on v4

--- a/solution.py
+++ b/solution.py
@@ -31,6 +31,17 @@
 
 def dot(a, b):
     return jnp.dot(a, b, preferred_element_type=F32)
+
+
+def piece_table(parts):
+    table = []
+    for p in range(parts):
+        sizes = (1, 1, 2, 2, 2) if p < parts - 1 else (2, 2, 2, 1, 1)
+        at = 0
+        for size in sizes:
+            table.append((p, at, size))
+            at += size
+    return table
 
 
 def remote(src, dst, send, recv, device):
@@ -94,7 +105,9 @@
     part = lax.rem(row, ratio)
     relays = block == col
     parts = chans // PART
-    pieces = parts * phases
+    table = piece_table(parts)
+    pieces = len(table)
+    of_part = lambda p: [k for k in range(pieces) if table[k][0] == p]
 
     for pad in (pad_one, pad_two):
         for at, size in ((0, chans), (depth + chans, chans)):
@@ -369,20 +382,23 @@
 
     def passes(d, k):
         target = lax.rem(col + d, cols)
-        straight_on = (k == pieces - 1) & crosses(target)
-        return jnp.logical_not(direct(col, target) | straight_on)
-
-    def band_of(k):
-        return pl.ds(pl.multiple_of((k // phases) * PART, PART), PART)
+        straight_on = direct(col, target)
+        if k == pieces - 1:
+            straight_on = straight_on | crosses(target) | (part == ratio - 1)
+        return jnp.logical_not(straight_on)
+
+    def span_of(k):
+        p, at, size = table[k]
+        return p, pl.ds(at, size)
 
     def source(h, k):
-        return summed.at[k % phases, :, band_of(k), pl.ds(h * height, height)]
+        return summed.at[(h, *span_of(k))]
 
     def landing(e, k):
-        return got.at[k % phases, pl.ds(e * count, count), band_of(k), :]
+        return got.at[(*span_of(k), pl.ds(e * count, count))]
 
     def waypoint(slot, k):
-        return relay.at[slot, k % phases, :, band_of(k), :]
+        return relay.at[(slot, *span_of(k))]
 
     def straight(h, k):
         return remote(
@@ -423,8 +439,10 @@
         )
 
     def issue(k):
-        goes = relays | mine | ((k == pieces - 1) & crosses(block))
         for h in range(ratio):
+            goes = relays | mine
+            if k == pieces - 1:
+                goes = goes | crosses(block) | (h == ratio - 1)
             here = relays & (part == h)
 
             @pl.when(goes & jnp.logical_not(here))
@@ -440,18 +458,20 @@
             at = pl.ds(phase * depth + q * chans, chans)
             cell = (held(at) - mean) * factor + shift
             cell = (x_ref[phase, pl.ds(q * chans, chans), :].astype(F32) + cell).astype(BF16)
-            summed[phase, q] = cell
+            for h in range(ratio):
+                for p in range(parts):
+                    summed[h, p, phase, q] = cell[
+                        p * PART : (p + 1) * PART, h * height : (h + 1) * height
+                    ]
             keep(at, cell.astype(F32))
-        issue(phase)
         return carry
 
-    lax.fori_loop(0, phases, finish, 0)
-
-    def issue_rest(k, carry):
+    for k in of_part(0):
+        _, at, size = table[k]
+        lax.fori_loop(at, at + size, finish, 0)
         issue(k)
-        return carry
-
-    lax.fori_loop(phases, pieces, issue_rest, 0)
+    for k in range(len(of_part(0)), pieces):
+        issue(k)
 
     @pl.when(relays)
     def _():
@@ -459,11 +479,9 @@
 
             @pl.when(part == h)
             def _(h=h):
-                got[:, pl.ds(h * count, count), :, :] = summed[
-                    :, :, :, pl.ds(h * height, height)
-                ]
-
-    def forward(k, carry):
+                got[:, :, pl.ds(h * count, count)] = summed[h]
+
+    def forward(k):
         for d in range(1, cols):
 
             @pl.when(passes(d, k))
@@ -479,7 +497,12 @@
                     ).wait_recv()
                     second_leg(d, e, k).start()
 
-        return carry
+    def drain(k):
+        for h in range(ratio):
+
+            @pl.when(jnp.logical_not(relays & (part == h)))
+            def _(h=h):
+                straight(h, k).wait_send()
 
     span = ratio * depth
     unit = one_hot(iota((height, height), 0) == iota((height, height), 1))
@@ -487,23 +510,29 @@
 
         @pl.when(relays)
         def _(p=p):
-            lax.fori_loop(p * phases, (p + 1) * phases, forward, 0)
+            for k in of_part(p):
+                forward(k)
+
+        if p > 0:
+            for k in of_part(p - 1):
+                drain(k)
 
         def collect(phase, carry, p=p):
-            k = p * phases + phase
-            for e in range(ratio):
-
-                @pl.when(jnp.logical_not(relays & (part == e)))
-                def _(e=e):
-                    arrive(e, k).wait_recv()
-
             for q in range(ratio * count):
                 wide[pl.ds(phase * span + q * chans + p * PART, PART), :] = got[
-                    phase, q, pl.ds(p * PART, PART), :
+                    p, phase, q
                 ].astype(F32)
             return carry
 
-        lax.fori_loop(0, phases, collect, 0)
+        for k in of_part(p):
+            for e in range(ratio):
+
+                @pl.when(jnp.logical_not(relays & (part == e)))
+                def _(e=e, k=k):
+                    arrive(e, k).wait_recv()
+
+            _, at, size = table[k]
+            lax.fori_loop(at, at + size, collect, 0)
 
         def turn(c, carry):
             own = jnp.concatenate(
@@ -528,30 +557,18 @@
 
         lax.fori_loop(p * PART, (p + 1) * PART, turn, 0, unroll=4)
 
-    def drain(k, carry):
-        for h in range(ratio):
-
-            @pl.when(jnp.logical_not(relays & (part == h)))
-            def _(h=h):
-                straight(h, k).wait_send()
-
-        return carry
-
-    lax.fori_loop(0, pieces, drain, 0)
+    for k in of_part(parts - 1):
+        drain(k)
 
     @pl.when(relays)
     def _():
-        def drain_relay(k, carry):
+        for k in range(pieces):
             for d in range(1, cols):
 
                 @pl.when(passes(d, k))
-                def _(d=d):
+                def _(d=d, k=k):
                     for e in range(ratio):
                         second_leg(d, e, k).wait_send()
-
-            return carry
-
-        lax.fori_loop(0, pieces, drain_relay, 0)
 
 
 def run(rows, cols, features, first, second, scales):
@@ -560,7 +577,8 @@
     depth = count * chans
     ratio = rows // cols
     slots = (cols - 1) * ratio
-    pieces = (chans // PART) * STEP
+    parts = chans // PART
+    pieces = len(piece_table(parts))
     full = depth + 2 * chans
     x = jnp.transpose(features.reshape(chans, count, STEP, width), (2, 1, 0, 3))
     x = x.reshape(STEP, depth, width)
@@ -583,10 +601,10 @@
             pltpu.VMEM((2, 2, depth // 2 + 2 * chans, LANES), BF16),
             pltpu.VMEM((2 * cols, 8, LANES), F32),
             pltpu.VMEM((2 * rows, 8, LANES), F32),
-            pltpu.VMEM((STEP, count, chans, width), BF16),
-            pltpu.VMEM((STEP, ratio * count, chans, height), BF16),
+            pltpu.VMEM((ratio, parts, STEP, count, PART, height), BF16),
+            pltpu.VMEM((parts, STEP, ratio * count, PART, height), BF16),
             pltpu.VMEM((STEP * ratio * depth, height), F32),
-            pltpu.VMEM((slots, STEP, count, chans, height), BF16),
+            pltpu.VMEM((slots, parts, STEP, count, PART, height), BF16),
             dma((16,)),
             dma((16,)),
             dma((2 * cols,)),

time: 93.7 us -> 93.1 us (level)
  no operation moved by 1% of the time
where the time goes in v5:
time: 93.1 us; the launch traced here: 93 us
  Pallas kernels  88.7 us (95%)
  local copies, waits for them, and re-layouts  4.2 us (5%)
    pallas_call x1, Pallas kernels, run(): pl.pallas_call(functools.partial(kernel, rows, cols), out_shape=jax.Shape...  88.7 us
    reshape x1, local copies, waits for them, and re-layouts, run(): x = jnp.transpose(features.reshape(chans, count, STEP, width), (2, 1, 0, 3))  2.86 us

profile of v5, /device:TPU:3, one launch (start us, length us, event | category | flops | bytes accessed | tf_op | source)
XLA Modules:
  0.0 93.0 jit_solution(4665679025406876512)
XLA Ops:
  0.0 0.0 copy-start
  0.0 0.0 copy-start.1
  0.0 0.0 copy-start.2
  0.0 0.0 copy-start.3
  0.0 0.0 copy-start.4
  0.0 0.0 copy-start.5
  0.0 2.9 %copy.8 = bf16[32,16,8,256]{3,0,1,2:T(8,128)(2,1)S(1)} copy(bf16[32,16,8,256]{3,2,1,0:T(8,128)(2,1)} %bitcast.13) | data formatting | bytes 4194304 | tf_op jit(solution)/shard_map/reshape | solution.py:583
  2.9 0.0 copy-done
  2.9 0.0 copy-done.1
  2.9 0.0 copy-done.2
  2.9 0.0 copy-done.3
  2.9 0.0 copy-done.4
  3.0 0.0 copy-done.5
  3.0 88.7 %shard_map.73 = bf16[32,128,256]{2,1,0:T(8,128)(2,1)S(1)} custom-call(bf16[8,512,256]{2,1,0:T(8,128)(2,1)S(1)} %bitcast.8, bf16[3,3,32,32]{3,2,1,0:T(8,128)(2,1)S(1)} %copy-done, bf16[3,3,32,32]{3,2,1,0:T(8,128)(2,1)S(1)} %copy-done.1, f32[1,32]{1,0:T(1,128)S(1)} %bitcast.9, f32[1,32]{1,0:T(1,128)S(1)} %bitcast.10, f32[1,32]{1,0:T(1,128)S(1)} %bitcast.11, ...), custom_call_target="tpu_custom_call" | custom-call | tf_op jit(solution)/shard_map/pallas_call | solution.py:588
  91.6 1.3 %copy.10 = bf16[32,128,256]{2,1,0:T(8,128)(2,1)} copy(bf16[32,128,256]{2,1,0:T(8,128)(2,1)S(1)} %shard_map.73) | data formatting | bytes 4194304
Async XLA Ops:
  0.0 2.9 %copy-start = (bf16[3,3,32,32]{3,2,1,0:T(8,128)(2,1)S(1)}, bf16[3,3,32,32]{3,2,1,0:T(8,128)(2,1)}, u32[]{:S(2)}) copy-start(bf16[3,3,32,32]{3,2,1,0:T(8,128)(2,1)} %first_ref.1) | copy-start | bytes 55300
  0.0 2.9 %copy-start.1 = (bf16[3,3,32,32]{3,2,1,0:T(8,128)(2,1)S(1)}, bf16[3,3,32,32]{3,2,1,0:T(8,128)(2,1)}, u32[]{:S(2)}) copy-start(bf16[3,3,32,32]{3,2,1,0:T(8,128)(2,1)} %second_ref.1) | copy-start | bytes 55300
  0.0 2.9 %copy-start.2 = (f32[32]{0:T(128)S(1)}, f32[32]{0:T(128)}, u32[]{:S(2)}) copy-start(f32[32]{0:T(128)} %param.10) | copy-start | bytes 388
  0.0 2.9 %copy-start.3 = (f32[32]{0:T(128)S(1)}, f32[32]{0:T(128)}, u32[]{:S(2)}) copy-start(f32[32]{0:T(128)} %param.11) | copy-start | bytes 388
  0.0 2.9 %copy-start.4 = (f32[32]{0:T(128)S(1)}, f32[32]{0:T(128)}, u32[]{:S(2)}) copy-start(f32[32]{0:T(128)} %param.12) | copy-start | bytes 388
  0.0 2.9 %copy-start.5 = (f32[32]{0:T(128)S(1)}, f32[32]{0:T(128)}, u32[]{:S(2)}) copy-start(f32[32]{0:T(128)} %param.13) | copy-start | bytes 388

commit v6 on v5

--- a/solution.py
+++ b/solution.py
@@ -142,7 +142,6 @@
         pl.when(jnp.logical_not(relays))(functools.partial(greet, (ratio * col + h, block)))
     expected = expected + jnp.where(relays, 0, ratio)
 
-    pad_one[:, pl.ds(chans, depth), :] = x_ref[...]
 
     i, j = iota((2 * LANES, LANES), 0), iota((2 * LANES, LANES), 1)
     edge = LANES - STEP
@@ -166,13 +165,13 @@
 
     pl.semaphore_wait(barrier, expected)
 
-    def halo_copy(pad, n, k):
+    def halo_copy(pad, n, k, own, base):
         dr, dc = WAYS[k]
         there, device = neighbour(k)
         if dc == 0:
-            source = chans if dr < 0 else depth
+            source = base if dr < 0 else base + depth - chans
             target = depth + chans if dr < 0 else 0
-            src = pad.at[:, pl.ds(source, chans)]
+            src = own.at[:, pl.ds(source, chans)]
             dst = pad.at[:, pl.ds(target, chans)]
         else:
             mine, theirs = (0, 1) if dc < 0 else (1, 0)
@@ -188,27 +187,27 @@
         slot = n * 8 + k
         return there, remote(src, dst, halo_send.at[slot], halo_recv.at[slot], device)
 
-    def halo_start(pad, n):
+    def halo_start(pad, n, own, base):
         for k in (1, 6):
-            there, copy = halo_copy(pad, n, k)
+            there, copy = halo_copy(pad, n, k, own, base)
             pl.when(there)(copy.start)
         for side, lane in ((0, 0), (1, width - LANES)):
             total = jnp.zeros((fold_rows, LANES), F32)
             for phase in range(phases):
-                low = pad[phase, pl.ds(chans, fold_rows), pl.ds(lane, LANES)]
-                high = pad[phase, pl.ds(chans + fold_rows, fold_rows), pl.ds(lane, LANES)]
+                low = own[phase, pl.ds(base, fold_rows), pl.ds(lane, LANES)]
+                high = own[phase, pl.ds(base + fold_rows, fold_rows), pl.ds(lane, LANES)]
                 total += dot(
                     jnp.concatenate([low, high], axis=1), pack_sel[side * phases + phase]
                 )
             packed[n, side] = total.astype(BF16)
             for k in (3, 0, 5) if side == 0 else (4, 2, 7):
-                there, copy = halo_copy(pad, n, k)
+                there, copy = halo_copy(pad, n, k, own, base)
                 pl.when(there)(copy.start)
 
     def halo_finish(pad, n):
         for k in range(8):
-            there, copy = halo_copy(pad, n, k)
-            _, back = halo_copy(pad, n, 7 - k)
+            there, copy = halo_copy(pad, n, k, pad, chans)
+            _, back = halo_copy(pad, n, 7 - k, pad, chans)
 
             @pl.when(there)
             def _(copy=copy, back=back):
@@ -352,7 +351,8 @@
         repeat = lambda v: jnp.concatenate([to_rows(v)] * (width // LANES), axis=1)
         return repeat(mean), repeat(factor), repeat(shifts)
 
-    halo_start(pad_one, 0)
+    halo_start(pad_one, 0, x_ref, 0)
+    pad_one[:, pl.ds(chans, depth), :] = x_ref[...]
     band(0, first_ref)
     band(1, second_ref)
     mean, factor, shift = norm(conv(pad_one, 0), 0, gain_one, shift_one)
@@ -364,8 +364,8 @@
             pad_two[phase, pl.ds((q + 1) * chans, chans), :] = cell.astype(BF16)
         return carry
 
-    lax.fori_loop(0, phases, activate, 0)
-    halo_start(pad_two, 1)
+    lax.fori_loop(0, phases, activate, 0, unroll=2)
+    halo_start(pad_two, 1, pad_two, chans)
     mean, factor, shift = norm(conv(pad_two, 1), 1, gain_two, shift_two)
 
     def direct(source_col, source_block):
@@ -599,8 +599,8 @@
             pltpu.VMEM((2, 3, GROUP * chans, (GROUP + 2) * chans), BF16),
             pltpu.VMEM((2, 2, depth // 2, LANES), BF16),
             pltpu.VMEM((2, 2, depth // 2 + 2 * chans, LANES), BF16),
-            pltpu.VMEM((2 * cols, 8, LANES), F32),
-            pltpu.VMEM((2 * rows, 8, LANES), F32),
+            pltpu.VMEM((2 * cols, 2, LANES), F32),
+            pltpu.VMEM((2 * rows, 2, LANES), F32),
             pltpu.VMEM((ratio, parts, STEP, count, PART, height), BF16),
             pltpu.VMEM((parts, STEP, ratio * count, PART, height), BF16),
             pltpu.VMEM((STEP * ratio * depth, height), F32),

time: 93.1 us -> 92.8 us (level)
  no operation moved by 1% of the time
where the time goes in v6:
time: 92.8 us; the launch traced here: 92.7 us
  Pallas kernels  88.4 us (95%)
  local copies, waits for them, and re-layouts  4.2 us (5%)
    pallas_call x1, Pallas kernels, run(): pl.pallas_call(functools.partial(kernel, rows, cols), out_shape=jax.Shape...  88.4 us
    reshape x1, local copies, waits for them, and re-layouts, run(): x = jnp.transpose(features.reshape(chans, count, STEP, width), (2, 1, 0, 3))  2.86 us

profile of v6, /device:TPU:3, one launch (start us, length us, event | category | flops | bytes accessed | tf_op | source)
XLA Modules:
  0.0 92.7 jit_solution(16922721550736278880)
XLA Ops:
  0.0 0.0 copy-start
  0.0 0.0 copy-start.1
  0.0 0.0 copy-start.2
  0.0 0.0 copy-start.3
  0.0 0.0 copy-start.4
  0.0 0.0 copy-start.5
  0.0 2.9 %copy.8 = bf16[32,16,8,256]{3,0,1,2:T(8,128)(2,1)S(1)} copy(bf16[32,16,8,256]{3,2,1,0:T(8,128)(2,1)} %bitcast.13) | data formatting | bytes 4194304 | tf_op jit(solution)/shard_map/reshape | solution.py:583
  2.9 0.0 copy-done
  2.9 0.0 copy-done.1
  2.9 0.0 copy-done.2
  2.9 0.0 copy-done.3
  2.9 0.0 copy-done.4
  3.0 0.0 copy-done.5
  3.0 88.4 %shard_map.73 = bf16[32,128,256]{2,1,0:T(8,128)(2,1)S(1)} custom-call(bf16[8,512,256]{2,1,0:T(8,128)(2,1)S(1)} %bitcast.8, bf16[3,3,32,32]{3,2,1,0:T(8,128)(2,1)S(1)} %copy-done, bf16[3,3,32,32]{3,2,1,0:T(8,128)(2,1)S(1)} %copy-done.1, f32[1,32]{1,0:T(1,128)S(1)} %bitcast.9, f32[1,32]{1,0:T(1,128)S(1)} %bitcast.10, f32[1,32]{1,0:T(1,128)S(1)} %bitcast.11, ...), custom_call_target="tpu_custom_call" | custom-call | tf_op jit(solution)/shard_map/pallas_call | solution.py:588
  91.4 1.3 %copy.10 = bf16[32,128,256]{2,1,0:T(8,128)(2,1)} copy(bf16[32,128,256]{2,1,0:T(8,128)(2,1)S(1)} %shard_map.73) | data formatting | bytes 4194304
Async XLA Ops:
  0.0 2.9 %copy-start = (bf16[3,3,32,32]{3,2,1,0:T(8,128)(2,1)S(1)}, bf16[3,3,32,32]{3,2,1,0:T(8,128)(2,1)}, u32[]{:S(2)}) copy-start(bf16[3,3,32,32]{3,2,1,0:T(8,128)(2,1)} %first_ref.1) | copy-start | bytes 55300
  0.0 2.9 %copy-start.1 = (bf16[3,3,32,32]{3,2,1,0:T(8,128)(2,1)S(1)}, bf16[3,3,32,32]{3,2,1,0:T(8,128)(2,1)}, u32[]{:S(2)}) copy-start(bf16[3,3,32,32]{3,2,1,0:T(8,128)(2,1)} %second_ref.1) | copy-start | bytes 55300
  0.0 2.9 %copy-start.2 = (f32[32]{0:T(128)S(1)}, f32[32]{0:T(128)}, u32[]{:S(2)}) copy-start(f32[32]{0:T(128)} %param.10) | copy-start | bytes 388
  0.0 2.9 %copy-start.3 = (f32[32]{0:T(128)S(1)}, f32[32]{0:T(128)}, u32[]{:S(2)}) copy-start(f32[32]{0:T(128)} %param.11) | copy-start | bytes 388
  0.0 2.9 %copy-start.4 = (f32[32]{0:T(128)S(1)}, f32[32]{0:T(128)}, u32[]{:S(2)}) copy-start(f32[32]{0:T(128)} %param.12) | copy-start | bytes 388
  0.0 2.9 %copy-start.5 = (f32[32]{0:T(128)S(1)}, f32[32]{0:T(128)}, u32[]{:S(2)}) copy-start(f32[32]{0:T(128)} %param.13) | copy-start | bytes 388

commit v7 on v6

--- a/solution.py
+++ b/solution.py
@@ -306,6 +306,8 @@
             )
             copy.start()
             copies.append(copy)
+        if n == 0 and not along_row:
+            band(1, second_ref)
         for copy in copies:
             copy.wait()
         means = [stats[base + d, pl.ds(0, 1), :] for d in range(axis_size)]
@@ -354,7 +356,6 @@
     halo_start(pad_one, 0, x_ref, 0)
     pad_one[:, pl.ds(chans, depth), :] = x_ref[...]
     band(0, first_ref)
-    band(1, second_ref)
     mean, factor, shift = norm(conv(pad_one, 0), 0, gain_one, shift_one)
 
     def activate(phase, carry):

time: 92.8 us -> 92.8 us (level)
  no operation moved by 1% of the time
where the time goes in v7:
time: 92.8 us; the launch traced here: 92.7 us
  Pallas kernels  88.4 us (95%)
  local copies, waits for them, and re-layouts  4.2 us (5%)
    pallas_call x1, Pallas kernels, run(): pl.pallas_call(functools.partial(kernel, rows, cols), out_shape=jax.Shape...  88.4 us
    reshape x1, local copies, waits for them, and re-layouts, run(): x = jnp.transpose(features.reshape(chans, count, STEP, width), (2, 1, 0, 3))  2.86 us

profile of v7, /device:TPU:3, one launch (start us, length us, event | category | flops | bytes accessed | tf_op | source)
XLA Modules:
  0.0 92.7 jit_solution(16532201446437285705)
XLA Ops:
  0.0 0.0 copy-start
  0.0 0.0 copy-start.1
  0.0 0.0 copy-start.2
  0.0 0.0 copy-start.3
  0.0 0.0 copy-start.4
  0.0 0.0 copy-start.5
  0.0 2.9 %copy.8 = bf16[32,16,8,256]{3,0,1,2:T(8,128)(2,1)S(1)} copy(bf16[32,16,8,256]{3,2,1,0:T(8,128)(2,1)} %bitcast.13) | data formatting | bytes 4194304 | tf_op jit(solution)/shard_map/reshape | solution.py:584
  2.9 0.0 copy-done
  2.9 0.0 copy-done.1
  2.9 0.0 copy-done.2
  2.9 0.0 copy-done.3
  2.9 0.0 copy-done.4
  3.0 0.0 copy-done.5
  3.0 88.4 %shard_map.73 = bf16[32,128,256]{2,1,0:T(8,128)(2,1)S(1)} custom-call(bf16[8,512,256]{2,1,0:T(8,128)(2,1)S(1)} %bitcast.8, bf16[3,3,32,32]{3,2,1,0:T(8,128)(2,1)S(1)} %copy-done, bf16[3,3,32,32]{3,2,1,0:T(8,128)(2,1)S(1)} %copy-done.1, f32[1,32]{1,0:T(1,128)S(1)} %bitcast.9, f32[1,32]{1,0:T(1,128)S(1)} %bitcast.10, f32[1,32]{1,0:T(1,128)S(1)} %bitcast.11, ...), custom_call_target="tpu_custom_call" | custom-call | tf_op jit(solution)/shard_map/pallas_call | solution.py:589
  91.4 1.3 %copy.10 = bf16[32,128,256]{2,1,0:T(8,128)(2,1)} copy(bf16[32,128,256]{2,1,0:T(8,128)(2,1)S(1)} %shard_map.73) | data formatting | bytes 4194304
Async XLA Ops:
  0.0 2.9 %copy-start = (bf16[3,3,32,32]{3,2,1,0:T(8,128)(2,1)S(1)}, bf16[3,3,32,32]{3,2,1,0:T(8,128)(2,1)}, u32[]{:S(2)}) copy-start(bf16[3,3,32,32]{3,2,1,0:T(8,128)(2,1)} %first_ref.1) | copy-start | bytes 55300
  0.0 2.9 %copy-start.1 = (bf16[3,3,32,32]{3,2,1,0:T(8,128)(2,1)S(1)}, bf16[3,3,32,32]{3,2,1,0:T(8,128)(2,1)}, u32[]{:S(2)}) copy-start(bf16[3,3,32,32]{3,2,1,0:T(8,128)(2,1)} %second_ref.1) | copy-start | bytes 55300
  0.0 2.9 %copy-start.2 = (f32[32]{0:T(128)S(1)}, f32[32]{0:T(128)}, u32[]{:S(2)}) copy-start(f32[32]{0:T(128)} %param.10) | copy-start | bytes 388
  0.0 2.9 %copy-start.3 = (f32[32]{0:T(128)S(1)}, f32[32]{0:T(128)}, u32[]{:S(2)}) copy-start(f32[32]{0:T(128)} %param.11) | copy-start | bytes 388
  0.0 2.9 %copy-start.4 = (f32[32]{0:T(128)S(1)}, f32[32]{0:T(128)}, u32[]{:S(2)}) copy-start(f32[32]{0:T(128)} %param.12) | copy-start | bytes 388
  0.0 2.9 %copy-start.5 = (f32[32]{0:T(128)S(1)}, f32[32]{0:T(128)}, u32[]{:S(2)}) copy-start(f32[32]{0:T(128)} %param.13) | copy-start | bytes 388

commit v8 on v7

--- a/solution.py
+++ b/solution.py
@@ -535,6 +535,10 @@
             _, at, size = table[k]
             lax.fori_loop(at, at + size, collect, 0)
 
+        if p == parts - 1:
+            for k in of_part(p)[:-2]:
+                drain(k)
+
         def turn(c, carry):
             own = jnp.concatenate(
                 [
@@ -558,7 +562,7 @@
 
         lax.fori_loop(p * PART, (p + 1) * PART, turn, 0, unroll=4)
 
-    for k in of_part(parts - 1):
+    for k in of_part(parts - 1)[-2:]:
         drain(k)
 
     @pl.when(relays)

time: 92.8 us -> 92.8 us (level)
  no operation moved by 1% of the time
where the time goes in v8:
time: 92.8 us; the launch traced here: 92.7 us
  Pallas kernels  88.4 us (95%)
  local copies, waits for them, and re-layouts  4.2 us (5%)
    pallas_call x1, Pallas kernels, run(): pl.pallas_call(functools.partial(kernel, rows, cols), out_shape=jax.Shape...  88.4 us
    reshape x1, local copies, waits for them, and re-layouts, run(): x = jnp.transpose(features.reshape(chans, count, STEP, width), (2, 1, 0, 3))  2.86 us

profile of v8, /device:TPU:3, one launch (start us, length us, event | category | flops | bytes accessed | tf_op | source)
XLA Modules:
  0.0 92.7 jit_solution(14600441912413679930)
XLA Ops:
  0.0 0.0 copy-start
  0.0 0.0 copy-start.1
  0.0 0.0 copy-start.2
  0.0 0.0 copy-start.3
  0.0 0.0 copy-start.4
  0.0 0.0 copy-start.5
  0.0 2.9 %copy.8 = bf16[32,16,8,256]{3,0,1,2:T(8,128)(2,1)S(1)} copy(bf16[32,16,8,256]{3,2,1,0:T(8,128)(2,1)} %bitcast.13) | data formatting | bytes 4194304 | tf_op jit(solution)/shard_map/reshape | solution.py:588
  2.9 0.0 copy-done
  2.9 0.0 copy-done.1
  2.9 0.0 copy-done.2
  2.9 0.0 copy-done.3
  2.9 0.0 copy-done.4
  3.0 0.0 copy-done.5
  3.0 88.4 %shard_map.73 = bf16[32,128,256]{2,1,0:T(8,128)(2,1)S(1)} custom-call(bf16[8,512,256]{2,1,0:T(8,128)(2,1)S(1)} %bitcast.8, bf16[3,3,32,32]{3,2,1,0:T(8,128)(2,1)S(1)} %copy-done, bf16[3,3,32,32]{3,2,1,0:T(8,128)(2,1)S(1)} %copy-done.1, f32[1,32]{1,0:T(1,128)S(1)} %bitcast.9, f32[1,32]{1,0:T(1,128)S(1)} %bitcast.10, f32[1,32]{1,0:T(1,128)S(1)} %bitcast.11, ...), custom_call_target="tpu_custom_call" | custom-call | tf_op jit(solution)/shard_map/pallas_call | solution.py:593
  91.4 1.3 %copy.10 = bf16[32,128,256]{2,1,0:T(8,128)(2,1)} copy(bf16[32,128,256]{2,1,0:T(8,128)(2,1)S(1)} %shard_map.73) | data formatting | bytes 4194304
Async XLA Ops:
  0.0 2.9 %copy-start = (bf16[3,3,32,32]{3,2,1,0:T(8,128)(2,1)S(1)}, bf16[3,3,32,32]{3,2,1,0:T(8,128)(2,1)}, u32[]{:S(2)}) copy-start(bf16[3,3,32,32]{3,2,1,0:T(8,128)(2,1)} %first_ref.1) | copy-start | bytes 55300
  0.0 2.9 %copy-start.1 = (bf16[3,3,32,32]{3,2,1,0:T(8,128)(2,1)S(1)}, bf16[3,3,32,32]{3,2,1,0:T(8,128)(2,1)}, u32[]{:S(2)}) copy-start(bf16[3,3,32,32]{3,2,1,0:T(8,128)(2,1)} %second_ref.1) | copy-start | bytes 55300
  0.0 2.9 %copy-start.2 = (f32[32]{0:T(128)S(1)}, f32[32]{0:T(128)}, u32[]{:S(2)}) copy-start(f32[32]{0:T(128)} %param.10) | copy-start | bytes 388
  0.0 2.9 %copy-start.3 = (f32[32]{0:T(128)S(1)}, f32[32]{0:T(128)}, u32[]{:S(2)}) copy-start(f32[32]{0:T(128)} %param.11) | copy-start | bytes 388
  0.0 2.9 %copy-start.4 = (f32[32]{0:T(128)S(1)}, f32[32]{0:T(128)}, u32[]{:S(2)}) copy-start(f32[32]{0:T(128)} %param.12) | copy-start | bytes 388
  0.0 2.9 %copy-start.5 = (f32[32]{0:T(128)S(1)}, f32[32]{0:T(128)}, u32[]{:S(2)}) copy-start(f32[32]{0:T(128)} %param.13) | copy-start | bytes 388
